TPU v7x, 32 devices: a whole 2x2x4 slice. The times are simulated.
32 devices in a mesh: fsdp: 8 (over z, y), seq: 4 (over x, core).
Axes of the slice: x: 2, y: 2, z: 4, core: 2. Of those that a mesh axis runs over, the one named last changes fastest.
Arguments:
- hidden_in: bfloat16 [32, 512, 768], P('fsdp', 'seq'), may hold values from -6 to 6
- encoder_states: bfloat16 [32, 256, 768], P('fsdp', 'seq'), may hold values from -6 to 6
- dec_segments: int32 [32, 512], P('fsdp', 'seq'), may hold values from 0 to 2, as said below
- enc_segments: int32 [32, 256], P('fsdp', 'seq'), may hold values from 0 to 2, as said below
- cotangent: bfloat16 [32, 512, 768], P('fsdp', 'seq'), may hold values from -6 to 6
- self_query: bfloat16 [768, 768], P(('fsdp', 'seq')), may hold values from -0.02734375 to 0.02734375
- self_key: bfloat16 [768, 768], P(('fsdp', 'seq')), may hold values from -0.21875 to 0.21875
- self_value: bfloat16 [768, 768], P(('fsdp', 'seq')), may hold values from -0.21875 to 0.21875
- self_output: bfloat16 [768, 768], P(('fsdp', 'seq')), may hold values from -0.875 to 0.875
- cross_query: bfloat16 [768, 768], P(('fsdp', 'seq')), may hold values from -0.02734375 to 0.02734375
- cross_key: bfloat16 [768, 768], P(('fsdp', 'seq')), may hold values from -0.21875 to 0.21875
- cross_value: bfloat16 [768, 768], P(('fsdp', 'seq')), may hold values from -0.21875 to 0.21875
- cross_output: bfloat16 [768, 768], P(('fsdp', 'seq')), may hold values from -0.875 to 0.875
- ffn_gate: bfloat16 [768, 2048], P(('fsdp', 'seq')), may hold values from -0.21875 to 0.21875
- ffn_up: bfloat16 [768, 2048], P(('fsdp', 'seq')), may hold values from -0.21875 to 0.21875
- ffn_down: bfloat16 [2048, 768], P(('fsdp', 'seq')), may hold values from -0.125 to 0.125
- norm_self: bfloat16 [768], P(('fsdp', 'seq')), may hold values from 0.5 to 1.5
- norm_cross: bfloat16 [768], P(('fsdp', 'seq')), may hold values from 0.5 to 1.5
- norm_ffn: bfloat16 [768], P(('fsdp', 'seq')), may hold values from 0.5 to 1.5
- bias_table: float32 [32, 12], P('seq'), may hold values from -4 to 4
Outputs:
- layer_out: bfloat16 [32, 512, 768], P('fsdp', 'seq')
- input_grad: bfloat16 [32, 512, 768], P('fsdp', 'seq')
- encoder_grad: bfloat16 [32, 256, 768], P('fsdp', 'seq')
- grad_self_query: float32 [768, 768], P(('fsdp', 'seq'))
- grad_self_key: float32 [768, 768], P(('fsdp', 'seq'))
- grad_self_value: float32 [768, 768], P(('fsdp', 'seq'))
- grad_self_output: float32 [768, 768], P(('fsdp', 'seq'))
- grad_cross_query: float32 [768, 768], P(('fsdp', 'seq'))
- grad_cross_key: float32 [768, 768], P(('fsdp', 'seq'))
- grad_cross_value: float32 [768, 768], P(('fsdp', 'seq'))
- grad_cross_output: float32 [768, 768], P(('fsdp', 'seq'))
- grad_ffn_gate: float32 [768, 2048], P(('fsdp', 'seq'))
- grad_ffn_up: float32 [768, 2048], P(('fsdp', 'seq'))
- grad_ffn_down: float32 [2048, 768], P(('fsdp', 'seq'))
- grad_norm_self: float32 [768], P(('fsdp', 'seq'))
- grad_norm_cross: float32 [768], P(('fsdp', 'seq'))
- grad_norm_ffn: float32 [768], P(('fsdp', 'seq'))
- grad_bias_table: float32 [32, 12], P('seq')
Inputs may be any that keep to these rules, and one draw needn't show every extreme that they name: `dec_segments`: along each row the numbers start at 0 and never fall; a row's decoder positions and its encoder states use the same set of numbers; in each aligned block of 4 rows one row holds a single document. `enc_segments`: along each row the numbers start at 0 and never fall, with the same set as the row's decoder positions.
All inputs are finite; a program needn't handle non-finite values.
Results may differ from a plain program's by a relative error of at most 0.023.
Values may be sent and summed in bfloat16 or wider, within the bound.
A program may use at most 192 MiB of HBM per device.

v0:
```python
from functools import partial
import math

import jax
import jax.numpy as jnp
from jax import lax
from jax.sharding import PartitionSpec as P

DH = 64
NB = 32


EPS = 1e-06
NEG_LARGE = -1000000000.0
HIGH = lax.Precision.HIGHEST
THRESHOLDS = (19, 21, 24, 27, 31, 35, 40, 46, 52, 59, 67, 77, 87, 99, 113)


def matmul(left, right):
    return jnp.dot(left, right, preferred_element_type=jnp.float32)


def matmul_left_t(left, right):
    return lax.dot_general(
        left, right, (((0,), (0,)), ((), ())), preferred_element_type=jnp.float32
    )


def matmul_right_t(left, right):
    return lax.dot_general(
        left, right, (((1,), (1,)), ((), ())), preferred_element_type=jnp.float32
    )


def bucket_table(query_pos, key_pos):
    distance = jnp.maximum(query_pos[:, None] - key_pos[None, :], 0)
    bucket_ids = jnp.minimum(distance, 16)
    for threshold in THRESHOLDS:
        bucket_ids = bucket_ids + (distance >= threshold).astype(jnp.int32)
    return (bucket_ids[:, :, None] == jnp.arange(NB)[None, None, :]).astype(jnp.float32)


def norm_forward(values, gain_vec):
    scale = lax.rsqrt(jnp.mean(values * values, axis=-1, keepdims=True) + EPS)
    unit = values * scale
    return ((unit * gain_vec).astype(jnp.bfloat16), unit, scale)


def norm_backward(grad_normed, unit, scale, gain_vec):
    grad_unit = grad_normed * gain_vec
    grad_gain = jnp.sum(grad_normed * unit, axis=0)
    grad_values = scale * (grad_unit - unit * jnp.mean(grad_unit * unit, axis=-1, keepdims=True))
    return (grad_values, grad_gain)


def attn_scores(queries, key_rows, allowed, pos_bias):
    scores = (
        jnp.einsum("bqhd,bkhd->bhqk", queries, key_rows, preferred_element_type=jnp.float32)
        + pos_bias
    )
    return jnp.where(allowed[:, None], scores, NEG_LARGE)


def attn_forward(queries, key_rows, value_rows, allowed, pos_bias):
    scores = attn_scores(queries, key_rows, allowed, pos_bias)
    top_score = jnp.max(scores, axis=-1, keepdims=True)
    expo = jnp.exp(scores - top_score)
    total = jnp.sum(expo, axis=-1, keepdims=True)
    attn_probs = (expo / total).astype(jnp.bfloat16)
    mixed = jnp.einsum(
        "bhqk,bkhd->bqhd", attn_probs, value_rows, preferred_element_type=jnp.float32
    )
    return (mixed, top_score + jnp.log(total))


def attn_query_side(queries, key_rows, value_rows, allowed, pos_bias, log_total, grad_mixed):
    scores = attn_scores(queries, key_rows, allowed, pos_bias)
    attn_probs = jnp.exp(scores - log_total)
    grad_probs = jnp.einsum(
        "bqhd,bkhd->bhqk", grad_mixed, value_rows, preferred_element_type=jnp.float32
    )
    row_stat = jnp.sum(grad_probs * attn_probs, axis=-1, keepdims=True)
    grad_scores = attn_probs * (grad_probs - row_stat)
    grad_low = grad_scores.astype(jnp.bfloat16)
    grad_query = jnp.einsum(
        "bhqk,bkhd->bqhd", grad_low, key_rows, preferred_element_type=jnp.float32
    )
    return (grad_query, grad_low, attn_probs, row_stat)


def attn_backward(queries, key_rows, value_rows, allowed, pos_bias, log_total, grad_mixed):
    grad_query, grad_low, attn_probs, row_stat = attn_query_side(
        queries, key_rows, value_rows, allowed, pos_bias, log_total, grad_mixed
    )
    grad_key = jnp.einsum("bhqk,bqhd->bkhd", grad_low, queries, preferred_element_type=jnp.float32)
    grad_value = jnp.einsum(
        "bhqk,bqhd->bkhd",
        attn_probs.astype(jnp.bfloat16),
        grad_mixed,
        preferred_element_type=jnp.float32,
    )
    return (grad_query, grad_key, grad_value, grad_low)


def per_device(
    hidden_in,
    encoder_states,
    dec_segments,
    enc_segments,
    cotangent,
    self_query,
    self_key,
    self_value,
    self_output,
    cross_query,
    cross_key,
    cross_value,
    cross_output,
    ffn_gate,
    ffn_up,
    ffn_down,
    norm_self,
    norm_cross,
    norm_ffn,
    bias_table,
):
    row_count, local_len, model_width = hidden_in.shape
    enc_local = encoder_states.shape[1]
    seq_size = lax.axis_size("seq")
    full_len = local_len * seq_size
    full_enc = enc_local * seq_size
    head_count = model_width // DH
    tokens = row_count * local_len
    shards = (
        self_query,
        self_key,
        self_value,
        self_output,
        cross_query,
        cross_key,
        cross_value,
        cross_output,
        ffn_gate,
        ffn_up,
        ffn_down,
        norm_self,
        norm_cross,
        norm_ffn,
    )
    gathered = (
        lax.all_gather(shards[0], ("fsdp", "seq"), axis=0, tiled=True),
        lax.all_gather(shards[1], ("fsdp", "seq"), axis=0, tiled=True),
        lax.all_gather(shards[2], ("fsdp", "seq"), axis=0, tiled=True),
        lax.all_gather(shards[3], ("fsdp", "seq"), axis=0, tiled=True),
        lax.all_gather(shards[4], ("fsdp", "seq"), axis=0, tiled=True),
        lax.all_gather(shards[5], ("fsdp", "seq"), axis=0, tiled=True),
        lax.all_gather(shards[6], ("fsdp", "seq"), axis=0, tiled=True),
        lax.all_gather(shards[7], ("fsdp", "seq"), axis=0, tiled=True),
        lax.all_gather(shards[8], ("fsdp", "seq"), axis=0, tiled=True),
        lax.all_gather(shards[9], ("fsdp", "seq"), axis=0, tiled=True),
        lax.all_gather(shards[10], ("fsdp", "seq"), axis=0, tiled=True),
        lax.all_gather(shards[11], ("fsdp", "seq"), axis=0, tiled=True),
        lax.all_gather(shards[12], ("fsdp", "seq"), axis=0, tiled=True),
        lax.all_gather(shards[13], ("fsdp", "seq"), axis=0, tiled=True),
    )
    (
        w_query,
        w_key,
        w_value,
        w_out_self,
        c_query_w,
        c_key_w,
        c_value_w,
        c_out_w,
        f_gate,
        f_up,
        f_down,
        g_self,
        g_cross,
        g_ffn,
    ) = gathered
    table_full, seg_float, enc_float = (
        lax.all_gather(bias_table, "seq", axis=0, tiled=True),
        lax.all_gather(dec_segments.astype(jnp.float32), "seq", axis=1, tiled=True),
        lax.all_gather(enc_segments.astype(jnp.float32), "seq", axis=1, tiled=True),
    )
    seg_rows = seg_float.astype(jnp.int32)
    enc_rows = enc_float.astype(jnp.int32)
    query_pos = lax.axis_index("seq") * local_len + jnp.arange(local_len)
    key_pos = jnp.arange(full_len)
    one_hot = bucket_table(query_pos, key_pos)
    pos_bias = jnp.einsum("qkn,nh->hqk", one_hot, table_full, precision=HIGH)
    causal = query_pos[:, None] >= key_pos[None, :]
    block_rows = math.gcd(row_count, max(1, 512 // local_len))
    blocks = row_count // block_rows

    def to_blocks(array_in):
        return array_in.reshape((blocks, block_rows) + array_in.shape[1:])

    x_flat = hidden_in.reshape(tokens, model_width).astype(jnp.float32)
    normed_self, unit_self, scale_self = norm_forward(x_flat, g_self)
    query_self = matmul(normed_self, w_query).astype(jnp.bfloat16)
    key_self = matmul(normed_self, w_key).astype(jnp.bfloat16)
    value_self = matmul(normed_self, w_value).astype(jnp.bfloat16)
    pair_self = jnp.stack([key_self, value_self]).reshape(2, row_count, local_len, model_width)
    pair_full = lax.all_gather(pair_self, "seq", axis=2, tiled=True)
    keys_full = pair_full[0].reshape(row_count, full_len, head_count, DH)
    values_full = pair_full[1].reshape(row_count, full_len, head_count, DH)
    queries_heads = query_self.reshape(row_count, local_len, head_count, DH)
    self_allowed = causal[None] & (dec_segments[:, :, None] == seg_rows[:, None, :])

    def self_forward(block_items):
        block_query, block_key, block_value, block_allowed = block_items
        return attn_forward(block_query, block_key, block_value, block_allowed, pos_bias)

    mixed_self, lse_self = lax.map(
        self_forward,
        (
            to_blocks(queries_heads),
            to_blocks(keys_full),
            to_blocks(values_full),
            to_blocks(self_allowed),
        ),
    )
    attn_self = mixed_self.reshape(tokens, model_width).astype(jnp.bfloat16)
    after_self = x_flat + matmul(attn_self, w_out_self)
    normed_cross, unit_cross, scale_cross = norm_forward(after_self, g_cross)
    query_cross = matmul(normed_cross, c_query_w).astype(jnp.bfloat16)
    states_full = lax.all_gather(encoder_states, "seq", axis=1, tiled=True)
    states_flat = states_full.reshape(row_count * full_enc, model_width)
    key_cross = (
        matmul(states_flat, c_key_w)
        .astype(jnp.bfloat16)
        .reshape(row_count, full_enc, head_count, DH)
    )
    value_cross = (
        matmul(states_flat, c_value_w)
        .astype(jnp.bfloat16)
        .reshape(row_count, full_enc, head_count, DH)
    )
    cross_heads = query_cross.reshape(row_count, local_len, head_count, DH)
    cross_allowed = dec_segments[:, :, None] == enc_rows[:, None, :]

    def cross_forward(block_items):
        block_query, block_key, block_value, block_allowed = block_items
        return attn_forward(block_query, block_key, block_value, block_allowed, 0.0)

    mixed_cross, lse_cross = lax.map(
        cross_forward,
        (
            to_blocks(cross_heads),
            to_blocks(key_cross),
            to_blocks(value_cross),
            to_blocks(cross_allowed),
        ),
    )
    attn_cross = mixed_cross.reshape(tokens, model_width).astype(jnp.bfloat16)
    after_cross = after_self + matmul(attn_cross, c_out_w)
    normed_ffn, unit_ffn, scale_ffn = norm_forward(after_cross, g_ffn)
    gate_pre = matmul(normed_ffn, f_gate)
    up_pre = matmul(normed_ffn, f_up)
    gate_act = jax.nn.gelu(gate_pre, approximate=True)
    hidden_units = (gate_act * up_pre).astype(jnp.bfloat16)
    layer_out = after_cross + matmul(hidden_units, f_down)
    regathered = (
        lax.all_gather(shards[0], ("fsdp", "seq"), axis=0, tiled=True),
        lax.all_gather(shards[1], ("fsdp", "seq"), axis=0, tiled=True),
        lax.all_gather(shards[2], ("fsdp", "seq"), axis=0, tiled=True),
        lax.all_gather(shards[3], ("fsdp", "seq"), axis=0, tiled=True),
        lax.all_gather(shards[4], ("fsdp", "seq"), axis=0, tiled=True),
        lax.all_gather(shards[5], ("fsdp", "seq"), axis=0, tiled=True),
        lax.all_gather(shards[6], ("fsdp", "seq"), axis=0, tiled=True),
        lax.all_gather(shards[7], ("fsdp", "seq"), axis=0, tiled=True),
        lax.all_gather(shards[8], ("fsdp", "seq"), axis=0, tiled=True),
        lax.all_gather(shards[9], ("fsdp", "seq"), axis=0, tiled=True),
        lax.all_gather(shards[10], ("fsdp", "seq"), axis=0, tiled=True),
        lax.all_gather(shards[11], ("fsdp", "seq"), axis=0, tiled=True),
        lax.all_gather(shards[12], ("fsdp", "seq"), axis=0, tiled=True),
        lax.all_gather(shards[13], ("fsdp", "seq"), axis=0, tiled=True),
    )
    (
        b_query,
        b_key,
        b_value,
        b_out_self,
        b_c_query,
        b_c_key,
        b_c_value,
        b_c_out,
        b_gate,
        b_up,
        b_down,
        b_g_self,
        b_g_cross,
        b_g_ffn,
    ) = regathered
    grad_top = cotangent.reshape(tokens, model_width).astype(jnp.float32)
    grad_top_low = grad_top.astype(jnp.bfloat16)
    grad_down_w = matmul_left_t(hidden_units, grad_top_low)
    grad_hidden = matmul_right_t(grad_top_low, b_down)
    gelu_value, gelu_pull = jax.vjp(partial(jax.nn.gelu, approximate=True), gate_pre)
    grad_gate = gelu_pull(grad_hidden * up_pre)[0].astype(jnp.bfloat16)
    grad_up = (grad_hidden * gate_act).astype(jnp.bfloat16)
    grad_gate_w = matmul_left_t(normed_ffn, grad_gate)
    grad_up_w = matmul_left_t(normed_ffn, grad_up)
    grad_normed_ffn = matmul_right_t(grad_gate, b_gate) + matmul_right_t(grad_up, b_up)
    grad_res_ffn, grad_g_ffn = norm_backward(grad_normed_ffn, unit_ffn, scale_ffn, b_g_ffn)
    grad_after_cross = grad_top + grad_res_ffn
    grad_cross_low = grad_after_cross.astype(jnp.bfloat16)
    grad_c_out = matmul_left_t(attn_cross, grad_cross_low)
    grad_attn_cross = (
        matmul_right_t(grad_cross_low, b_c_out)
        .astype(jnp.bfloat16)
        .reshape(row_count, local_len, head_count, DH)
    )

    def cross_back(block_items):
        block_query, block_key, block_value, block_allowed, block_lse, block_grad = block_items
        grad_query, grad_key, grad_value, grad_low = attn_backward(
            block_query, block_key, block_value, block_allowed, 0.0, block_lse, block_grad
        )
        return (grad_query, grad_key, grad_value)

    grad_qc, grad_kc, grad_vc = lax.map(
        cross_back,
        (
            to_blocks(cross_heads),
            to_blocks(key_cross),
            to_blocks(value_cross),
            to_blocks(cross_allowed),
            lse_cross,
            to_blocks(grad_attn_cross),
        ),
    )
    grad_pair_cross = jnp.stack(
        [
            grad_kc.reshape(row_count, full_enc, model_width),
            grad_vc.reshape(row_count, full_enc, model_width),
        ]
    )
    summed_cross = lax.psum_scatter(
        grad_pair_cross.astype(jnp.bfloat16), "seq", scatter_dimension=2, tiled=True
    ).astype(jnp.float32)
    grad_kc_low = summed_cross[0].reshape(row_count * enc_local, model_width).astype(jnp.bfloat16)
    grad_vc_low = summed_cross[1].reshape(row_count * enc_local, model_width).astype(jnp.bfloat16)
    states_local = encoder_states.reshape(row_count * enc_local, model_width)
    grad_c_key = matmul_left_t(states_local, grad_kc_low)
    grad_c_value = matmul_left_t(states_local, grad_vc_low)
    grad_states = matmul_right_t(grad_kc_low, b_c_key) + matmul_right_t(grad_vc_low, b_c_value)
    grad_qc_low = grad_qc.reshape(tokens, model_width).astype(jnp.bfloat16)
    grad_c_query = matmul_left_t(normed_cross, grad_qc_low)
    grad_normed_cross = matmul_right_t(grad_qc_low, b_c_query)
    grad_res_cross, grad_g_cross = norm_backward(
        grad_normed_cross, unit_cross, scale_cross, b_g_cross
    )
    grad_after_self = grad_after_cross + grad_res_cross
    grad_self_low = grad_after_self.astype(jnp.bfloat16)
    grad_out_self_w = matmul_left_t(attn_self, grad_self_low)
    grad_attn_self = (
        matmul_right_t(grad_self_low, b_out_self)
        .astype(jnp.bfloat16)
        .reshape(row_count, local_len, head_count, DH)
    )

    def self_back(block_items):
        block_query, block_key, block_value, block_allowed, block_lse, block_grad = block_items
        grad_query, grad_key, grad_value, grad_low = attn_backward(
            block_query, block_key, block_value, block_allowed, pos_bias, block_lse, block_grad
        )
        bias_part = jnp.einsum(
            "hqk,qkn->nh", jnp.sum(grad_low.astype(jnp.float32), axis=0), one_hot, precision=HIGH
        )
        return (grad_query, grad_key, grad_value, bias_part)

    grad_qs, grad_ks, grad_vs, bias_parts = lax.map(
        self_back,
        (
            to_blocks(queries_heads),
            to_blocks(keys_full),
            to_blocks(values_full),
            to_blocks(self_allowed),
            lse_self,
            to_blocks(grad_attn_self),
        ),
    )
    grad_pair_self = jnp.stack(
        [
            grad_ks.reshape(row_count, full_len, model_width),
            grad_vs.reshape(row_count, full_len, model_width),
        ]
    )
    summed_self = lax.psum_scatter(
        grad_pair_self.astype(jnp.bfloat16), "seq", scatter_dimension=2, tiled=True
    ).astype(jnp.float32)
    grad_key_low = summed_self[0].reshape(tokens, model_width).astype(jnp.bfloat16)
    grad_value_low = summed_self[1].reshape(tokens, model_width).astype(jnp.bfloat16)
    grad_query_low = grad_qs.reshape(tokens, model_width).astype(jnp.bfloat16)
    grad_q_w = matmul_left_t(normed_self, grad_query_low)
    grad_k_w = matmul_left_t(normed_self, grad_key_low)
    grad_v_w = matmul_left_t(normed_self, grad_value_low)
    grad_normed_self = (
        matmul_right_t(grad_query_low, b_query)
        + matmul_right_t(grad_key_low, b_key)
        + matmul_right_t(grad_value_low, b_value)
    )
    grad_res_self, grad_g_self = norm_backward(grad_normed_self, unit_self, scale_self, b_g_self)
    grad_input = grad_after_self + grad_res_self
    grads_sharded = (
        lax.psum_scatter(grad_q_w, ("fsdp", "seq"), scatter_dimension=0, tiled=True),
        lax.psum_scatter(grad_k_w, ("fsdp", "seq"), scatter_dimension=0, tiled=True),
        lax.psum_scatter(grad_v_w, ("fsdp", "seq"), scatter_dimension=0, tiled=True),
        lax.psum_scatter(grad_out_self_w, ("fsdp", "seq"), scatter_dimension=0, tiled=True),
        lax.psum_scatter(grad_c_query, ("fsdp", "seq"), scatter_dimension=0, tiled=True),
        lax.psum_scatter(grad_c_key, ("fsdp", "seq"), scatter_dimension=0, tiled=True),
        lax.psum_scatter(grad_c_value, ("fsdp", "seq"), scatter_dimension=0, tiled=True),
        lax.psum_scatter(grad_c_out, ("fsdp", "seq"), scatter_dimension=0, tiled=True),
        lax.psum_scatter(grad_gate_w, ("fsdp", "seq"), scatter_dimension=0, tiled=True),
        lax.psum_scatter(grad_up_w, ("fsdp", "seq"), scatter_dimension=0, tiled=True),
        lax.psum_scatter(grad_down_w, ("fsdp", "seq"), scatter_dimension=0, tiled=True),
        lax.psum_scatter(grad_g_self, ("fsdp", "seq"), scatter_dimension=0, tiled=True),
        lax.psum_scatter(grad_g_cross, ("fsdp", "seq"), scatter_dimension=0, tiled=True),
        lax.psum_scatter(grad_g_ffn, ("fsdp", "seq"), scatter_dimension=0, tiled=True),
    )
    bias_total = lax.psum(jnp.sum(bias_parts, axis=0), ("fsdp", "seq"))
    bias_share = NB // seq_size
    bias_grad = lax.dynamic_slice_in_dim(
        bias_total, lax.axis_index("seq") * bias_share, bias_share, 0
    )
    return (
        layer_out.reshape(row_count, local_len, model_width).astype(jnp.bfloat16),
        grad_input.reshape(row_count, local_len, model_width).astype(jnp.bfloat16),
        grad_states.reshape(row_count, enc_local, model_width).astype(jnp.bfloat16),
        grads_sharded[0],
        grads_sharded[1],
        grads_sharded[2],
        grads_sharded[3],
        grads_sharded[4],
        grads_sharded[5],
        grads_sharded[6],
        grads_sharded[7],
        grads_sharded[8],
        grads_sharded[9],
        grads_sharded[10],
        grads_sharded[11],
        grads_sharded[12],
        grads_sharded[13],
        bias_grad,
    )


def solution(mesh):
    return jax.shard_map(
        per_device,
        mesh=mesh,
        in_specs=(
            P("fsdp", "seq", None),
            P("fsdp", "seq", None),
            P("fsdp", "seq"),
            P("fsdp", "seq"),
            P("fsdp", "seq", None),
            P(("fsdp", "seq"), None),
            P(("fsdp", "seq"), None),
            P(("fsdp", "seq"), None),
            P(("fsdp", "seq"), None),
            P(("fsdp", "seq"), None),
            P(("fsdp", "seq"), None),
            P(("fsdp", "seq"), None),
            P(("fsdp", "seq"), None),
            P(("fsdp", "seq"), None),
            P(("fsdp", "seq"), None),
            P(("fsdp", "seq"), None),
            P(("fsdp", "seq")),
            P(("fsdp", "seq")),
            P(("fsdp", "seq")),
            P("seq", None),
        ),
        out_specs=(
            P("fsdp", "seq", None),
            P("fsdp", "seq", None),
            P("fsdp", "seq", None),
            P(("fsdp", "seq"), None),
            P(("fsdp", "seq"), None),
            P(("fsdp", "seq"), None),
            P(("fsdp", "seq"), None),
            P(("fsdp", "seq"), None),
            P(("fsdp", "seq"), None),
            P(("fsdp", "seq"), None),
            P(("fsdp", "seq"), None),
            P(("fsdp", "seq"), None),
            P(("fsdp", "seq"), None),
            P(("fsdp", "seq"), None),
            P(("fsdp", "seq")),
            P(("fsdp", "seq")),
            P(("fsdp", "seq")),
            P("seq", None),
        ),
        check_vma=False,
    )
```

profile of v0, /device:TPU:0, one launch (start us, length us, event | category | flops | bytes accessed | tf_op | source)
XLA Modules:
  0.0 2067.7 jit_solution(4696911410703970863)
XLA Ops:
  13.7 42.2 %all-reduce.7 = (bf16[768]{0:T(1024)(128)(2,1)S(1)}, bf16[768]{0:T(1024)(128)(2,1)S(1)}, bf16[768]{0:T(1024)(128)(2,1)S(1)}) all-reduce(bf16[768]{0:T(1024)(128)(2,1)S(1)} %dynamic-update-slice, bf16[768]{0:T(1024)(128)(2,1)S(1)} %dynamic-update-slice.1, ...), channel_id=1, replica_groups=mesh['fsdp'=8,'seq'=4] {'fsdp','seq'}, use_global_device_ids=true, to_apply=%add | all-reduce | flops 2304 | bytes 9216
  59.8 7.9 all-gather.17.cloned.1.call-done
  69.8 53.8 %all-gather.15.cloned.1.call-done = bf16[768,768]{1,0:T(8,128)(2,1)} async-done(((bf16[24,768]{1,0:T(8,128)(2,1)}), bf16[768,768]{1,0:T(8,128)(2,1)}) %all-gather.15.cloned.1.call-update) | async-done | bytes 1179664 | tf_op jit(solution)/shard_map/all_gather | solution.py:152
  148.8 37.7 %copy.96 = pred[128,512,32]{1,2,0:T(32,128)(4,1)S(1)} copy(pred[128,512,32]{0,2,1:T(32,128)(4,1)S(1)} %iota_compare_fusion) | data formatting | bytes 4194304 | tf_op jit(solution)/shard_map/eq | solution.py:40
  196.4 38.9 %all-gather.27.cloned.1.call-done = bf16[768,768]{1,0:T(8,128)(2,1)} async-done(((bf16[24,768]{1,0:T(8,128)(2,1)}), bf16[768,768]{1,0:T(8,128)(2,1)}) %all-gather.27.cloned.1.call-update) | async-done | bytes 1179664 | tf_op jit(solution)/shard_map/all_gather | solution.py:157
  235.3 20.0 all-gather.25.cloned.1.call-done
  261.6 50.5 %all-gather.31.cloned.1.call-done = bf16[768,768]{1,0:T(8,128)(2,1)} async-done(((bf16[24,768]{1,0:T(8,128)(2,1)}), bf16[768,768]{1,0:T(8,128)(2,1)}) %all-gather.31.cloned.1.call-update) | async-done | bytes 1179664 | tf_op jit(solution)/shard_map/all_gather | solution.py:156
  318.4 40.6 %all-gather.19.cloned.1.call-done = bf16[2,4,512,768]{3,2,1,0:T(8,128)(2,1)} async-done(((bf16[2,4,128,768]{3,2,1,0:T(8,128)(2,1)}), bf16[2,4,512,768]{3,2,1,0:T(8,128)(2,1)}) %all-gather.19.cloned.1.call-update) | async-done | bytes 6291472 | tf_op jit(solution)/shard_map/all_gather | solution.py:206
  389.0 27.0 %all-gather.23.cloned.1.call-done = bf16[768,768]{1,0:T(8,128)(2,1)} async-done(((bf16[24,768]{1,0:T(8,128)(2,1)}), bf16[768,768]{1,0:T(8,128)(2,1)}) %all-gather.23.cloned.1.call-update) | async-done | bytes 1179664 | tf_op jit(solution)/shard_map/all_gather | solution.py:154
  418.3 53.7 %all-gather.29.cloned.1.call-done = bf16[768,768]{1,0:T(8,128)(2,1)} async-done(((bf16[24,768]{1,0:T(8,128)(2,1)}), bf16[768,768]{1,0:T(8,128)(2,1)}) %all-gather.29.cloned.1.call-update) | async-done | bytes 1179664 | tf_op jit(solution)/shard_map/all_gather | solution.py:155
  484.1 43.6 %all-gather.33.cloned.1.call-done = bf16[768,768]{1,0:T(8,128)(2,1)} async-done(((bf16[24,768]{1,0:T(8,128)(2,1)}), bf16[768,768]{1,0:T(8,128)(2,1)}) %all-gather.33.cloned.1.call-update) | async-done | bytes 1179664 | tf_op jit(solution)/shard_map/all_gather | solution.py:158
  531.3 57.2 %all-gather.37.cloned.1.call-done = bf16[768,2048]{1,0:T(8,128)(2,1)} async-done(((bf16[24,2048]{1,0:T(8,128)(2,1)}), bf16[768,2048]{1,0:T(8,128)(2,1)}) %all-gather.37.cloned.1.call-update) | async-done | bytes 3145744 | tf_op jit(solution)/shard_map/all_gather | solution.py:160
  594.2 54.7 %all-gather.35.cloned.1.call-done = bf16[768,2048]{1,0:T(8,128)(2,1)} async-done(((bf16[24,2048]{1,0:T(8,128)(2,1)}), bf16[768,2048]{1,0:T(8,128)(2,1)}) %all-gather.35.cloned.1.call-update) | async-done | bytes 3145744 | tf_op jit(solution)/shard_map/all_gather | solution.py:159
  654.7 55.0 %all-gather.39.cloned.1.call-done = bf16[2048,768]{1,0:T(8,128)(2,1)} async-done(((bf16[64,768]{1,0:T(8,128)(2,1)}), bf16[2048,768]{1,0:T(8,128)(2,1)}) %all-gather.39.cloned.1.call-update) | async-done | bytes 3145744 | tf_op jit(solution)/shard_map/all_gather | solution.py:161
  709.6 8.7 multiply_convert_fusion.2
  765.8 7.4 fusion.21
  778.3 7.3 multiply_reduce_fusion
  785.6 8.7 convert_reduce_fusion
  856.6 9.1 reduce-scatter.18.cloned.1.call-done
  880.6 6.9 convolution_bitcast_fusion.3
  896.8 39.7 %all-reduce.6 = (f32[768]{0:T(1024)S(1)}, f32[768]{0:T(1024)S(1)}, f32[768]{0:T(1024)S(1)}, f32[32,12]{1,0:T(8,128)S(1)}) all-reduce(f32[768]{0:T(1024)S(1)} %get-tuple-element.190, f32[768]{0:T(1024)S(1)} %get-tuple-element.188, f32[768]{0:T(1024)S(1)} %get-tuple-element.186, ...), channel_id=15, replica_groups=mesh['fsdp'=8,'seq'=4] {'fsdp','seq'}, use_global_device_ids=true, to_apply=%region_26.27.clone | all-reduce | flops 2688 | bytes 21504
  941.7 28.9 %reduce-scatter.32.cloned.1.call-done = f32[24,768]{1,0:T(8,128)} async-done(((f32[768,768]{1,0:T(8,128)}), f32[24,768]{1,0:T(8,128)}) %reduce-scatter.32.cloned.1.call-update) | async-done | bytes 73744 | tf_op jit(solution)/shard_map/reduce_scatter | solution.py:416
  970.5 104.7 %reduce-scatter.30.cloned.1.call-done = f32[24,768]{1,0:T(8,128)} async-done(((f32[768,768]{1,0:T(8,128)}), f32[24,768]{1,0:T(8,128)}) %reduce-scatter.30.cloned.1.call-update) | async-done | bytes 73744 | tf_op jit(solution)/shard_map/reduce_scatter | solution.py:413
  1075.2 103.7 %reduce-scatter.28.cloned.1.call-done = f32[24,768]{1,0:T(8,128)} async-done(((f32[768,768]{1,0:T(8,128)}), f32[24,768]{1,0:T(8,128)}) %reduce-scatter.28.cloned.1.call-update) | async-done | bytes 73744 | tf_op jit(solution)/shard_map/reduce_scatter | solution.py:412
  1178.9 104.8 %reduce-scatter.22.cloned.1.call-done = f32[24,768]{1,0:T(8,128)} async-done(((f32[768,768]{1,0:T(8,128)}), f32[24,768]{1,0:T(8,128)}) %reduce-scatter.22.cloned.1.call-update) | async-done | bytes 73744 | tf_op jit(solution)/shard_map/reduce_scatter | solution.py:409
  1283.7 119.4 %reduce-scatter.36.cloned.1.call-done = f32[24,2048]{1,0:T(8,128)} async-done(((f32[768,2048]{1,0:T(8,128)}), f32[24,2048]{1,0:T(8,128)}) %reduce-scatter.36.cloned.1.call-update) | async-done | bytes 196624 | tf_op jit(solution)/shard_map/reduce_scatter | solution.py:418
  1403.0 120.7 %reduce-scatter.34.cloned.1.call-done = f32[24,2048]{1,0:T(8,128)} async-done(((f32[768,2048]{1,0:T(8,128)}), f32[24,2048]{1,0:T(8,128)}) %reduce-scatter.34.cloned.1.call-update) | async-done | bytes 196624 | tf_op jit(solution)/shard_map/reduce_scatter | solution.py:417
  1523.7 119.7 %reduce-scatter.38.cloned.1.call-done = f32[64,768]{1,0:T(8,128)} async-done(((f32[2048,768]{1,0:T(8,128)}), f32[64,768]{1,0:T(8,128)}) %reduce-scatter.38.cloned.1.call-update) | async-done | bytes 196624 | tf_op jit(solution)/shard_map/reduce_scatter | solution.py:419
  1643.5 105.0 %reduce-scatter.42.cloned.1.call-done = f32[24,768]{1,0:T(8,128)} async-done(((f32[768,768]{1,0:T(8,128)}), f32[24,768]{1,0:T(8,128)}) %reduce-scatter.42.cloned.1.call-update) | async-done | bytes 73744
  1748.5 103.7 %reduce-scatter.40.cloned.1.call-done = f32[24,768]{1,0:T(8,128)} async-done(((f32[768,768]{1,0:T(8,128)}), f32[24,768]{1,0:T(8,128)}) %reduce-scatter.40.cloned.1.call-update) | async-done | bytes 73744
  1852.2 104.8 %reduce-scatter.26.cloned.1.call-done = f32[24,768]{1,0:T(8,128)} async-done(((f32[768,768]{1,0:T(8,128)}), f32[24,768]{1,0:T(8,128)}) %reduce-scatter.26.cloned.1.call-update) | async-done | bytes 73744 | tf_op jit(solution)/shard_map/reduce_scatter | solution.py:411
  1957.0 103.8 %reduce-scatter.24.cloned.1.call-done = f32[24,768]{1,0:T(8,128)} async-done(((f32[768,768]{1,0:T(8,128)}), f32[24,768]{1,0:T(8,128)}) %reduce-scatter.24.cloned.1.call-update) | async-done | bytes 73744 | tf_op jit(solution)/shard_map/reduce_scatter | solution.py:410
  (329 shorter events, 262.5 us)
Async XLA Ops:
  7.2 60.5 %all-gather.17.cloned.1.call-start = ((), (), s32[]{:S(2)}) async-start(), calls=%async_computation.14 | async-start | bytes 1216512 | tf_op jit(solution)/shard_map/all_gather | solution.py:153
  7.9 115.7 %all-gather.15.cloned.1.call-start = ((), (), s32[]{:S(2)}) async-start(), calls=%async_computation.13 | async-start | bytes 1216512 | tf_op jit(solution)/shard_map/all_gather | solution.py:152
  8.7 184.3 %all-gather.21.cloned.1.call-start = ((), (), s32[]{:S(2)}) async-start(), calls=%async_computation.16 | async-start | bytes 1216512 | tf_op jit(solution)/shard_map/all_gather | solution.py:151
  9.4 225.9 %all-gather.27.cloned.1.call-start = ((), (), s32[]{:S(2)}) async-start(), calls=%async_computation.19 | async-start | bytes 1216512 | tf_op jit(solution)/shard_map/all_gather | solution.py:157
  10.0 245.3 %all-gather.25.cloned.1.call-start = ((), (), s32[]{:S(2)}) async-start(), calls=%async_computation.18 | async-start | bytes 1966080 | tf_op jit(solution)/shard_map/all_gather | solution.py:229
  10.6 301.6 %all-gather.31.cloned.1.call-start = ((), (), s32[]{:S(2)}) async-start(), calls=%async_computation.21 | async-start | bytes 1216512 | tf_op jit(solution)/shard_map/all_gather | solution.py:156
  11.1 347.9 %all-gather.19.cloned.1.call-start = ((), (), s32[]{:S(2)}) async-start(), calls=%async_computation.15 | async-start | bytes 7864320 | tf_op jit(solution)/shard_map/all_gather | solution.py:206
  127.0 289.1 %all-gather.23.cloned.1.call-start = ((), (), s32[]{:S(2)}) async-start(), calls=%async_computation.17 | async-start | bytes 1216512 | tf_op jit(solution)/shard_map/all_gather | solution.py:154
  127.7 344.2 %all-gather.29.cloned.1.call-start = ((), (), s32[]{:S(2)}) async-start(), calls=%async_computation.20 | async-start | bytes 1216512 | tf_op jit(solution)/shard_map/all_gather | solution.py:155
  128.4 399.3 %all-gather.33.cloned.1.call-start = ((), (), s32[]{:S(2)}) async-start(), calls=%async_computation.22 | async-start | bytes 1216512 | tf_op jit(solution)/shard_map/all_gather | solution.py:158
  129.0 459.4 %all-gather.37.cloned.1.call-start = ((), (), s32[]{:S(2)}) async-start(), calls=%async_computation.24 | async-start | bytes 3244032 | tf_op jit(solution)/shard_map/all_gather | solution.py:160
  129.8 519.2 %all-gather.35.cloned.1.call-start = ((), (), s32[]{:S(2)}) async-start(), calls=%async_computation.23 | async-start | bytes 3244032 | tf_op jit(solution)/shard_map/all_gather | solution.py:159
  130.3 579.3 %all-gather.39.cloned.1.call-start = ((), (), s32[]{:S(2)}) async-start(), calls=%async_computation.25 | async-start | bytes 3244032 | tf_op jit(solution)/shard_map/all_gather | solution.py:161
  131.1 719.1 %reduce-scatter.20.cloned.1.call-start = ((), (), s32[]{:S(2)}) async-start(), calls=%async_computation.27 | async-start | bytes 3932160 | tf_op jit(solution)/shard_map/reduce_scatter | solution.py:341
  131.7 54.9 %copy-start.47 = (s32[128,512]{0,1:T(8,128)}, s32[128,512]{0,1:T(8,128)S(1)}, u32[]{:S(2)}) copy-start(s32[128,512]{0,1:T(8,128)S(1)} %convert_add_fusion) | copy-start | bytes 786436
  418.3 109.5 %copy-start.11 = (f32[512,768]{1,0:T(8,128)}, f32[512,768]{1,0:T(8,128)S(1)}, u32[]{:S(2)}) copy-start(f32[512,768]{1,0:T(8,128)S(1)} %get-tuple-element.215) | copy-start | bytes 4718596
  484.1 45.8 %copy-start.28 = (bf16[4,128,12,64]{1,0,3,2:T(4,128)(2,1)}, bf16[4,128,12,64]{1,0,3,2:T(4,128)(2,1)S(1)}, u32[]{:S(2)}) copy-start(bf16[4,128,12,64]{1,0,3,2:T(4,128)(2,1)S(1)} %copy.106) | copy-start | bytes 2359300
  531.3 117.7 %copy-start.30 = (bf16[512,768]{1,0:T(8,128)(2,1)}, bf16[512,768]{1,0:T(8,128)(2,1)S(1)}, u32[]{:S(2)}) copy-start(bf16[512,768]{1,0:T(8,128)(2,1)S(1)} %multiply_convert_fusion.4) | copy-start | bytes 2359300
  594.2 115.4 %copy-start.41 = (bf16[4,128,768]{2,1,0:T(8,128)(2,1)S(1)}, bf16[4,128,768]{2,1,0:T(8,128)(2,1)}, u32[]{:S(2)}) copy-start(bf16[4,128,768]{2,1,0:T(8,128)(2,1)} %param.24) | copy-start | bytes 2359300
  757.2 108.5 %reduce-scatter.18.cloned.1.call-start = ((), (), s32[]{:S(2)}) async-start(), calls=%async_computation.26 | async-start | bytes 7864320 | tf_op jit(solution)/shard_map/reduce_scatter | solution.py:392
  807.9 162.6 %reduce-scatter.32.cloned.1.call-start = ((), (), s32[]{:S(2)}) async-start(), calls=%async_computation.33 | async-start | bytes 2433024 | tf_op jit(solution)/shard_map/reduce_scatter | solution.py:416
  811.7 263.4 %reduce-scatter.30.cloned.1.call-start = ((), (), s32[]{:S(2)}) async-start(), calls=%async_computation.32 | async-start | bytes 2433024 | tf_op jit(solution)/shard_map/reduce_scatter | solution.py:413
  816.5 362.4 %reduce-scatter.28.cloned.1.call-start = ((), (), s32[]{:S(2)}) async-start(), calls=%async_computation.31 | async-start | bytes 2433024 | tf_op jit(solution)/shard_map/reduce_scatter | solution.py:412
  820.9 462.7 %reduce-scatter.22.cloned.1.call-start = ((), (), s32[]{:S(2)}) async-start(), calls=%async_computation.28 | async-start | bytes 2433024 | tf_op jit(solution)/shard_map/reduce_scatter | solution.py:409
  832.1 570.9 %reduce-scatter.36.cloned.1.call-start = ((), (), s32[]{:S(2)}) async-start(), calls=%async_computation.35 | async-start | bytes 6488064 | tf_op jit(solution)/shard_map/reduce_scatter | solution.py:418
  837.7 686.0 %reduce-scatter.34.cloned.1.call-start = ((), (), s32[]{:S(2)}) async-start(), calls=%async_computation.34 | async-start | bytes 6488064 | tf_op jit(solution)/shard_map/reduce_scatter | solution.py:417
  843.9 799.6 %reduce-scatter.38.cloned.1.call-start = ((), (), s32[]{:S(2)}) async-start(), calls=%async_computation.36 | async-start | bytes 6488064 | tf_op jit(solution)/shard_map/reduce_scatter | solution.py:419
  850.1 898.3 %reduce-scatter.42.cloned.1.call-start = ((), (), s32[]{:S(2)}) async-start(), calls=%async_computation.38 | async-start | bytes 2433024
  854.0 998.2 %reduce-scatter.40.cloned.1.call-start = ((), (), s32[]{:S(2)}) async-start(), calls=%async_computation.37 | async-start | bytes 2433024
  856.5 1100.4 %reduce-scatter.26.cloned.1.call-start = ((), (), s32[]{:S(2)}) async-start(), calls=%async_computation.30 | async-start | bytes 2433024 | tf_op jit(solution)/shard_map/reduce_scatter | solution.py:411
  869.5 1191.2 %reduce-scatter.24.cloned.1.call-start = ((), (), s32[]{:S(2)}) async-start(), calls=%async_computation.29 | async-start | bytes 2433024 | tf_op jit(solution)/shard_map/reduce_scatter | solution.py:410
  894.4 44.4 %copy-start.19 = (f32[512,768]{1,0:T(8,128)S(1)}, f32[512,768]{1,0:T(8,128)}, u32[]{:S(2)}) copy-start(f32[512,768]{1,0:T(8,128)} %copy-done.17) | copy-start | bytes 4718596
  (70 other events, 303.1 us)
Sparse Core Ops, SparseCore 0:
  10.9 56.7 all-gather.16
  70.6 52.9 all-gather.14
  126.5 53.0 all-gather.20
  182.3 52.9 all-gather.26
  236.7 18.5 all-gather.24
  258.1 54.0 all-gather.30
  313.7 45.3 all-gather.18
  361.9 54.0 all-gather.22
  419.0 52.9 all-gather.28
  474.7 52.9 all-gather.32
  530.6 57.8 all-gather.36
  591.2 57.7 all-gather.34
  651.8 57.7 all-gather.38
  757.3 36.7 reduce-scatter.19
  808.1 57.5 reduce-scatter.17
  871.4 99.0 reduce-scatter.31
  977.1 98.0 reduce-scatter.29
  1080.9 97.9 reduce-scatter.27
  1185.6 98.0 reduce-scatter.21
  1289.7 113.2 reduce-scatter.35
  1410.2 113.4 reduce-scatter.33
  1529.9 113.4 reduce-scatter.37
  1650.2 98.2 reduce-scatter.41
  1754.2 97.9 reduce-scatter.39
  1858.9 97.9 reduce-scatter.25
  1962.7 97.9 reduce-scatter.23
where the time goes:
time: 2070 us
  waiting for transfers between devices  1640 us (79%)
  matrix products  147 us (7%)
  local copies, waits for them, and re-layouts  127 us (6%)
  blocking collectives  97.3 us (5%)
  other arithmetic  40.7 us (2%)
    unnamed x28, waiting for transfers between devices  216 us
    reduce_scatter x1, waiting for transfers between devices, per_device(): lax.psum_scatter(grad_gate_w, ('fsdp', 'seq'), scatter_dimension=0, tiled...  121 us
    reduce_scatter x1, waiting for transfers between devices, per_device(): lax.psum_scatter(grad_down_w, ('fsdp', 'seq'), scatter_dimension=0, tiled...  120 us
    reduce_scatter x1, waiting for transfers between devices, per_device(): lax.psum_scatter(grad_up_w, ('fsdp', 'seq'), scatter_dimension=0, tiled=T...  119 us
    reduce_scatter x1, waiting for transfers between devices, per_device(): lax.psum_scatter(grad_q_w, ('fsdp', 'seq'), scatter_dimension=0, tiled=True)  105 us
    reduce_scatter x1, waiting for transfers between devices, per_device(): lax.psum_scatter(grad_v_w, ('fsdp', 'seq'), scatter_dimension=0, tiled=True)  105 us
    reduce_scatter x1, waiting for transfers between devices, per_device(): lax.psum_scatter(grad_c_query, ('fsdp', 'seq'), scatter_dimension=0, tile...  105 us
    reduce_scatter x1, waiting for transfers between devices, per_device(): lax.psum_scatter(grad_k_w, ('fsdp', 'seq'), scatter_dimension=0, tiled=True)  104 us
  transfers between devices with their start and end apart: 26, of which 24 were waited for; matrix products, arithmetic and copies ran while one was open for 12% of the time, Pallas kernels for 0%

commit v1 on v0

--- a/solution.py
+++ b/solution.py
@@ -37,7 +37,7 @@
     bucket_ids = jnp.minimum(distance, 16)
     for threshold in THRESHOLDS:
         bucket_ids = bucket_ids + (distance >= threshold).astype(jnp.int32)
-    return (bucket_ids[:, :, None] == jnp.arange(NB)[None, None, :]).astype(jnp.float32)
+    return (bucket_ids[None] == jnp.arange(NB)[:, None, None]).astype(jnp.float32)
 
 
 def norm_forward(values, gain_vec):
@@ -131,65 +131,68 @@
     full_enc = enc_local * seq_size
     head_count = model_width // DH
     tokens = row_count * local_len
-    shards = (
-        self_query,
-        self_key,
-        self_value,
-        self_output,
-        cross_query,
-        cross_key,
-        cross_value,
-        cross_output,
-        ffn_gate,
-        ffn_up,
-        ffn_down,
-        norm_self,
-        norm_cross,
-        norm_ffn,
-    )
-    gathered = (
-        lax.all_gather(shards[0], ("fsdp", "seq"), axis=0, tiled=True),
-        lax.all_gather(shards[1], ("fsdp", "seq"), axis=0, tiled=True),
-        lax.all_gather(shards[2], ("fsdp", "seq"), axis=0, tiled=True),
-        lax.all_gather(shards[3], ("fsdp", "seq"), axis=0, tiled=True),
-        lax.all_gather(shards[4], ("fsdp", "seq"), axis=0, tiled=True),
-        lax.all_gather(shards[5], ("fsdp", "seq"), axis=0, tiled=True),
-        lax.all_gather(shards[6], ("fsdp", "seq"), axis=0, tiled=True),
-        lax.all_gather(shards[7], ("fsdp", "seq"), axis=0, tiled=True),
-        lax.all_gather(shards[8], ("fsdp", "seq"), axis=0, tiled=True),
-        lax.all_gather(shards[9], ("fsdp", "seq"), axis=0, tiled=True),
-        lax.all_gather(shards[10], ("fsdp", "seq"), axis=0, tiled=True),
-        lax.all_gather(shards[11], ("fsdp", "seq"), axis=0, tiled=True),
-        lax.all_gather(shards[12], ("fsdp", "seq"), axis=0, tiled=True),
-        lax.all_gather(shards[13], ("fsdp", "seq"), axis=0, tiled=True),
-    )
-    (
-        w_query,
-        w_key,
-        w_value,
-        w_out_self,
-        c_query_w,
-        c_key_w,
-        c_value_w,
-        c_out_w,
-        f_gate,
-        f_up,
-        f_down,
-        g_self,
-        g_cross,
-        g_ffn,
-    ) = gathered
-    table_full, seg_float, enc_float = (
-        lax.all_gather(bias_table, "seq", axis=0, tiled=True),
-        lax.all_gather(dec_segments.astype(jnp.float32), "seq", axis=1, tiled=True),
-        lax.all_gather(enc_segments.astype(jnp.float32), "seq", axis=1, tiled=True),
-    )
-    seg_rows = seg_float.astype(jnp.int32)
-    enc_rows = enc_float.astype(jnp.int32)
+    axes = ("fsdp", "seq")
+    total_devices = lax.axis_size("fsdp") * seq_size
+    shard_rows = self_query.shape[0]
+    down_rows, hidden_width = ffn_down.shape[0], ffn_gate.shape[1]
+    folds = -(-down_rows // shard_rows)
+    down_padded = jnp.pad(ffn_down, ((0, folds * shard_rows - down_rows), (0, 0)))
+    gains = jnp.pad(jnp.stack([norm_self, norm_cross, norm_ffn], axis=1), ((0, 0), (0, 125)))
+    first_pack = jnp.concatenate([self_query, self_key, self_value, gains], axis=1)
+    rest_pack = jnp.concatenate(
+        [self_output, cross_query, cross_key, cross_value, cross_output, ffn_gate, ffn_up]
+        + [down_padded[i * shard_rows : (i + 1) * shard_rows] for i in range(folds)],
+        axis=1,
+    )
+    first_full = lax.all_gather(first_pack, axes, axis=0, tiled=True)
+    w_qkv = first_full[:, : 3 * model_width]
+    gain_rows = first_full[:, 3 * model_width : 3 * model_width + 3].astype(jnp.float32)
+    g_self, g_cross, g_ffn = gain_rows[:, 0], gain_rows[:, 1], gain_rows[:, 2]
+    buckets_local = bias_table.shape[0]
+    bias_high = bias_table.astype(jnp.bfloat16)
+    bias_low = (bias_table - bias_high.astype(jnp.float32)).astype(jnp.bfloat16)
+    bias_size = buckets_local * head_count
+    side_parts = jnp.concatenate(
+        [
+            dec_segments.astype(jnp.bfloat16),
+            enc_segments.astype(jnp.bfloat16),
+            jnp.broadcast_to(bias_high.reshape(1, bias_size), (row_count, bias_size)),
+            jnp.broadcast_to(bias_low.reshape(1, bias_size), (row_count, bias_size)),
+        ],
+        axis=1,
+    )
+    side_pad = jnp.pad(side_parts, ((0, 0), (0, model_width - side_parts.shape[1])))
+    side_block = jnp.pad(side_pad[:, None, :], ((0, 0), (0, 15), (0, 0)))
+    states_pack = jnp.concatenate([encoder_states, side_block], axis=1)
+    states_gathered = lax.all_gather(states_pack, "seq", axis=1, tiled=False)
+    states_full = states_gathered[:, :, :enc_local].reshape(row_count, full_enc, model_width)
+    side_full = states_gathered[:, :, enc_local].astype(jnp.float32)
+    seg_rows = side_full[:, :, :local_len].reshape(row_count, full_len).astype(jnp.int32)
+    side_at = local_len + enc_local
+    enc_rows = side_full[:, :, local_len:side_at].reshape(row_count, full_enc).astype(jnp.int32)
+    table_full = (
+        side_full[0, :, side_at : side_at + bias_size]
+        + side_full[0, :, side_at + bias_size : side_at + 2 * bias_size]
+    ).reshape(seq_size * buckets_local, head_count)
+    rest_full = lax.all_gather(rest_pack, axes, axis=0, tiled=True)
+    cuts = [model_width] * 5 + [hidden_width] * 2
+    pieces, at = [], 0
+    for width in cuts:
+        pieces.append(rest_full[:, at : at + width])
+        at += width
+    w_out_self, c_query_w, c_key_w, c_value_w, c_out_w, f_gate, f_up = pieces
+    down_folds = rest_full[:, at:].reshape(total_devices, shard_rows, folds, model_width)
+    f_down = jnp.concatenate(
+        [
+            down_folds[:, : min(shard_rows, down_rows - i * shard_rows), i]
+            for i in range(folds)
+        ],
+        axis=1,
+    ).reshape(total_devices * down_rows, model_width)
     query_pos = lax.axis_index("seq") * local_len + jnp.arange(local_len)
     key_pos = jnp.arange(full_len)
     one_hot = bucket_table(query_pos, key_pos)
-    pos_bias = jnp.einsum("qkn,nh->hqk", one_hot, table_full, precision=HIGH)
+    pos_bias = jnp.einsum("nqk,nh->hqk", one_hot, table_full, precision=HIGH)
     causal = query_pos[:, None] >= key_pos[None, :]
     block_rows = math.gcd(row_count, max(1, 512 // local_len))
     blocks = row_count // block_rows
@@ -199,9 +202,10 @@
 
     x_flat = hidden_in.reshape(tokens, model_width).astype(jnp.float32)
     normed_self, unit_self, scale_self = norm_forward(x_flat, g_self)
-    query_self = matmul(normed_self, w_query).astype(jnp.bfloat16)
-    key_self = matmul(normed_self, w_key).astype(jnp.bfloat16)
-    value_self = matmul(normed_self, w_value).astype(jnp.bfloat16)
+    qkv_self = matmul(normed_self, w_qkv).astype(jnp.bfloat16)
+    query_self = qkv_self[:, :model_width]
+    key_self = qkv_self[:, model_width : 2 * model_width]
+    value_self = qkv_self[:, 2 * model_width :]
     pair_self = jnp.stack([key_self, value_self]).reshape(2, row_count, local_len, model_width)
     pair_full = lax.all_gather(pair_self, "seq", axis=2, tiled=True)
     keys_full = pair_full[0].reshape(row_count, full_len, head_count, DH)
@@ -226,7 +230,6 @@
     after_self = x_flat + matmul(attn_self, w_out_self)
     normed_cross, unit_cross, scale_cross = norm_forward(after_self, g_cross)
     query_cross = matmul(normed_cross, c_query_w).astype(jnp.bfloat16)
-    states_full = lax.all_gather(encoder_states, "seq", axis=1, tiled=True)
     states_flat = states_full.reshape(row_count * full_enc, model_width)
     key_cross = (
         matmul(states_flat, c_key_w)
@@ -262,54 +265,41 @@
     gate_act = jax.nn.gelu(gate_pre, approximate=True)
     hidden_units = (gate_act * up_pre).astype(jnp.bfloat16)
     layer_out = after_cross + matmul(hidden_units, f_down)
-    regathered = (
-        lax.all_gather(shards[0], ("fsdp", "seq"), axis=0, tiled=True),
-        lax.all_gather(shards[1], ("fsdp", "seq"), axis=0, tiled=True),
-        lax.all_gather(shards[2], ("fsdp", "seq"), axis=0, tiled=True),
-        lax.all_gather(shards[3], ("fsdp", "seq"), axis=0, tiled=True),
-        lax.all_gather(shards[4], ("fsdp", "seq"), axis=0, tiled=True),
-        lax.all_gather(shards[5], ("fsdp", "seq"), axis=0, tiled=True),
-        lax.all_gather(shards[6], ("fsdp", "seq"), axis=0, tiled=True),
-        lax.all_gather(shards[7], ("fsdp", "seq"), axis=0, tiled=True),
-        lax.all_gather(shards[8], ("fsdp", "seq"), axis=0, tiled=True),
-        lax.all_gather(shards[9], ("fsdp", "seq"), axis=0, tiled=True),
-        lax.all_gather(shards[10], ("fsdp", "seq"), axis=0, tiled=True),
-        lax.all_gather(shards[11], ("fsdp", "seq"), axis=0, tiled=True),
-        lax.all_gather(shards[12], ("fsdp", "seq"), axis=0, tiled=True),
-        lax.all_gather(shards[13], ("fsdp", "seq"), axis=0, tiled=True),
-    )
-    (
-        b_query,
-        b_key,
-        b_value,
-        b_out_self,
-        b_c_query,
-        b_c_key,
-        b_c_value,
-        b_c_out,
-        b_gate,
-        b_up,
-        b_down,
-        b_g_self,
-        b_g_cross,
-        b_g_ffn,
-    ) = regathered
     grad_top = cotangent.reshape(tokens, model_width).astype(jnp.float32)
     grad_top_low = grad_top.astype(jnp.bfloat16)
     grad_down_w = matmul_left_t(hidden_units, grad_top_low)
-    grad_hidden = matmul_right_t(grad_top_low, b_down)
+    grad_hidden = matmul_right_t(grad_top_low, f_down)
     gelu_value, gelu_pull = jax.vjp(partial(jax.nn.gelu, approximate=True), gate_pre)
     grad_gate = gelu_pull(grad_hidden * up_pre)[0].astype(jnp.bfloat16)
     grad_up = (grad_hidden * gate_act).astype(jnp.bfloat16)
     grad_gate_w = matmul_left_t(normed_ffn, grad_gate)
     grad_up_w = matmul_left_t(normed_ffn, grad_up)
-    grad_normed_ffn = matmul_right_t(grad_gate, b_gate) + matmul_right_t(grad_up, b_up)
-    grad_res_ffn, grad_g_ffn = norm_backward(grad_normed_ffn, unit_ffn, scale_ffn, b_g_ffn)
+    down_split = grad_down_w.astype(jnp.bfloat16).reshape(total_devices, down_rows, model_width)
+    down_split = jnp.pad(down_split, ((0, 0), (0, folds * shard_rows - down_rows), (0, 0)))
+    ffn_pack = jnp.concatenate(
+        [grad_gate_w.astype(jnp.bfloat16), grad_up_w.astype(jnp.bfloat16)]
+        + [
+            down_split[:, i * shard_rows : (i + 1) * shard_rows].reshape(model_width, model_width)
+            for i in range(folds)
+        ],
+        axis=1,
+    )
+    ffn_summed = lax.psum_scatter(ffn_pack, axes, scatter_dimension=0, tiled=True)
+    ffn_summed = ffn_summed.astype(jnp.float32)
+    down_share = jnp.concatenate(
+        [
+            ffn_summed[:, 2 * hidden_width + i * model_width :][:, :model_width]
+            for i in range(folds)
+        ],
+        axis=0,
+    )[:down_rows]
+    grad_normed_ffn = matmul_right_t(grad_gate, f_gate) + matmul_right_t(grad_up, f_up)
+    grad_res_ffn, grad_g_ffn = norm_backward(grad_normed_ffn, unit_ffn, scale_ffn, g_ffn)
     grad_after_cross = grad_top + grad_res_ffn
     grad_cross_low = grad_after_cross.astype(jnp.bfloat16)
     grad_c_out = matmul_left_t(attn_cross, grad_cross_low)
     grad_attn_cross = (
-        matmul_right_t(grad_cross_low, b_c_out)
+        matmul_right_t(grad_cross_low, c_out_w)
         .astype(jnp.bfloat16)
         .reshape(row_count, local_len, head_count, DH)
     )
@@ -346,18 +336,18 @@
     states_local = encoder_states.reshape(row_count * enc_local, model_width)
     grad_c_key = matmul_left_t(states_local, grad_kc_low)
     grad_c_value = matmul_left_t(states_local, grad_vc_low)
-    grad_states = matmul_right_t(grad_kc_low, b_c_key) + matmul_right_t(grad_vc_low, b_c_value)
+    grad_states = matmul_right_t(grad_kc_low, c_key_w) + matmul_right_t(grad_vc_low, c_value_w)
     grad_qc_low = grad_qc.reshape(tokens, model_width).astype(jnp.bfloat16)
     grad_c_query = matmul_left_t(normed_cross, grad_qc_low)
-    grad_normed_cross = matmul_right_t(grad_qc_low, b_c_query)
+    grad_normed_cross = matmul_right_t(grad_qc_low, c_query_w)
     grad_res_cross, grad_g_cross = norm_backward(
-        grad_normed_cross, unit_cross, scale_cross, b_g_cross
+        grad_normed_cross, unit_cross, scale_cross, g_cross
     )
     grad_after_self = grad_after_cross + grad_res_cross
     grad_self_low = grad_after_self.astype(jnp.bfloat16)
     grad_out_self_w = matmul_left_t(attn_self, grad_self_low)
     grad_attn_self = (
-        matmul_right_t(grad_self_low, b_out_self)
+        matmul_right_t(grad_self_low, w_out_self)
         .astype(jnp.bfloat16)
         .reshape(row_count, local_len, head_count, DH)
     )
@@ -368,7 +358,7 @@
             block_query, block_key, block_value, block_allowed, pos_bias, block_lse, block_grad
         )
         bias_part = jnp.einsum(
-            "hqk,qkn->nh", jnp.sum(grad_low.astype(jnp.float32), axis=0), one_hot, precision=HIGH
+            "hqk,nqk->nh", jnp.sum(grad_low.astype(jnp.float32), axis=0), one_hot, precision=HIGH
         )
         return (grad_query, grad_key, grad_value, bias_part)
 
@@ -398,33 +388,55 @@
     grad_q_w = matmul_left_t(normed_self, grad_query_low)
     grad_k_w = matmul_left_t(normed_self, grad_key_low)
     grad_v_w = matmul_left_t(normed_self, grad_value_low)
-    grad_normed_self = (
-        matmul_right_t(grad_query_low, b_query)
-        + matmul_right_t(grad_key_low, b_key)
-        + matmul_right_t(grad_value_low, b_value)
-    )
-    grad_res_self, grad_g_self = norm_backward(grad_normed_self, unit_self, scale_self, b_g_self)
+    grad_normed_self = matmul_right_t(
+        jnp.concatenate([grad_query_low, grad_key_low, grad_value_low], axis=1), w_qkv
+    )
+    grad_res_self, grad_g_self = norm_backward(grad_normed_self, unit_self, scale_self, g_self)
     grad_input = grad_after_self + grad_res_self
+    bias_total = jnp.sum(bias_parts, axis=0)
+    bias_columns = -(-bias_size // shard_rows)
+    bias_spread = jnp.pad(
+        bias_total.reshape(seq_size, bias_size),
+        ((0, 0), (0, bias_columns * shard_rows - bias_size)),
+    ).reshape(1, seq_size * shard_rows, bias_columns)
+    fsdp_size = lax.axis_size("fsdp")
+    bias_spread = jnp.broadcast_to(
+        bias_spread, (fsdp_size, seq_size * shard_rows, bias_columns)
+    ).reshape(model_width, bias_columns)
+    small = jnp.concatenate(
+        [jnp.stack([grad_g_self, grad_g_cross, grad_g_ffn], axis=1), bias_spread], axis=1
+    )
+    small = jnp.pad(small, ((0, 0), (0, 256 - small.shape[1])))
+    late_pack = jnp.concatenate(
+        [
+            part.astype(jnp.bfloat16)
+            for part in (
+                grad_q_w,
+                grad_k_w,
+                grad_v_w,
+                grad_out_self_w,
+                grad_c_query,
+                grad_c_key,
+                grad_c_value,
+                grad_c_out,
+                small,
+            )
+        ],
+        axis=1,
+    )
+    late_summed = lax.psum_scatter(late_pack, axes, scatter_dimension=0, tiled=True)
+    late_summed = late_summed.astype(jnp.float32)
+    small_summed = late_summed[:, 8 * model_width :]
+    bias_sum = small_summed[:, 3 : 3 + bias_columns].reshape(-1)[:bias_size]
+    bias_grad = bias_sum.reshape(buckets_local, head_count)
     grads_sharded = (
-        lax.psum_scatter(grad_q_w, ("fsdp", "seq"), scatter_dimension=0, tiled=True),
-        lax.psum_scatter(grad_k_w, ("fsdp", "seq"), scatter_dimension=0, tiled=True),
-        lax.psum_scatter(grad_v_w, ("fsdp", "seq"), scatter_dimension=0, tiled=True),
-        lax.psum_scatter(grad_out_self_w, ("fsdp", "seq"), scatter_dimension=0, tiled=True),
-        lax.psum_scatter(grad_c_query, ("fsdp", "seq"), scatter_dimension=0, tiled=True),
-        lax.psum_scatter(grad_c_key, ("fsdp", "seq"), scatter_dimension=0, tiled=True),
-        lax.psum_scatter(grad_c_value, ("fsdp", "seq"), scatter_dimension=0, tiled=True),
-        lax.psum_scatter(grad_c_out, ("fsdp", "seq"), scatter_dimension=0, tiled=True),
-        lax.psum_scatter(grad_gate_w, ("fsdp", "seq"), scatter_dimension=0, tiled=True),
-        lax.psum_scatter(grad_up_w, ("fsdp", "seq"), scatter_dimension=0, tiled=True),
-        lax.psum_scatter(grad_down_w, ("fsdp", "seq"), scatter_dimension=0, tiled=True),
-        lax.psum_scatter(grad_g_self, ("fsdp", "seq"), scatter_dimension=0, tiled=True),
-        lax.psum_scatter(grad_g_cross, ("fsdp", "seq"), scatter_dimension=0, tiled=True),
-        lax.psum_scatter(grad_g_ffn, ("fsdp", "seq"), scatter_dimension=0, tiled=True),
-    )
-    bias_total = lax.psum(jnp.sum(bias_parts, axis=0), ("fsdp", "seq"))
-    bias_share = NB // seq_size
-    bias_grad = lax.dynamic_slice_in_dim(
-        bias_total, lax.axis_index("seq") * bias_share, bias_share, 0
+        *(late_summed[:, i * model_width : (i + 1) * model_width] for i in range(8)),
+        ffn_summed[:, :hidden_width],
+        ffn_summed[:, hidden_width : 2 * hidden_width],
+        down_share,
+        small_summed[:, 0],
+        small_summed[:, 1],
+        small_summed[:, 2],
     )
     return (
         layer_out.reshape(row_count, local_len, model_width).astype(jnp.bfloat16),

time: 2070 us -> 796 us (0.38)
  waiting for transfers between devices: 1640 us -> 397 us
  blocking collectives: 97.3 us -> 0 us
  local copies, waits for them, and re-layouts: 127 us -> 188 us
    reduce_scatter x9 -> x1, waiting for transfers between devices: 910 us -> 92.2 us  [per_device(): lax.psum_scatter(ffn_pack, axes, scatter_dimension=0, tiled=True)]
    all_gather x12 -> x3, waiting for transfers between devices: 462 us -> 141 us  [the longest x1 82 us: per_device(): rest_full = lax.all_gather(rest_pack, axes, axis=0, tiled=True)]
    unnamed x2 -> x0, blocking collectives: 81.9 us -> none
    unnamed x28 -> x9, waiting for transfers between devices: 216 us -> 140 us
    all_gather x1, waiting for transfers between devices: 40.6 us -> 9.06 us  [per_device(): pair_full = lax.all_gather(pair_self, 'seq', axis=2, tiled=True)]
    slice x1 -> x16, local copies, waits for them, and re-layouts: 1.47 us -> 28 us  [the longest x2 15.7 us: per_device(): down_folds[:, :min(shard_rows, down_rows - i * shard_rows), i]]
    unnamed x163 -> x213, local copies, waits for them, and re-layouts: 33.1 us -> 53.5 us
  transfers between devices with their start and end apart: 26 -> 8, of which waited for: 24 -> 6; matrix products, arithmetic and copies ran while one was open for 12% -> 30% of each run, Pallas kernels for 0% -> 0%
where the time goes in v1:
time: 796 us; the launch traced here: 790 us
  waiting for transfers between devices  397 us (50%)
  local copies, waits for them, and re-layouts  188 us (24%)
  matrix products  137 us (17%)
  other arithmetic  50.6 us (6%)
  between operations  16 us (2%)
    unnamed x9, waiting for transfers between devices  140 us
    reduce_scatter x1, waiting for transfers between devices, per_device(): lax.psum_scatter(ffn_pack, axes, scatter_dimension=0, tiled=True)  92.2 us
    all_gather x1, waiting for transfers between devices, per_device(): rest_full = lax.all_gather(rest_pack, axes, axis=0, tiled=True)  82 us
    all_gather x1, waiting for transfers between devices, per_device(): first_full = lax.all_gather(first_pack, axes, axis=0, tiled=True)  58.9 us
    unnamed x213, local copies, waits for them, and re-layouts  53.5 us
    eq x1, local copies, waits for them, and re-layouts, bucket_table(): bucket_ids[None] == jnp.arange(NB)[:, None, None]  37.8 us
    dot_general x9, matrix products, matmul(): return jnp.dot(left, right, preferred_element_type=jnp.float32)  30.2 us
    dot_general x11, matrix products, matmul_left_t(): lax.dot_general(left, right, (((0,), (0,)), ((), ())), preferred_element_...  24.9 us
  transfers between devices with their start and end apart: 8, of which 6 were waited for; matrix products, arithmetic and copies ran while one was open for 30% of the time, Pallas kernels for 0%

profile of v1, /device:TPU:0, one launch (start us, length us, event | category | flops | bytes accessed | tf_op | source)
XLA Modules:
  0.0 789.8 jit_solution(13786847953679420382)
XLA Ops:
  16.0 58.9 %all-gather.6.cloned.1.call-done = bf16[768,2432]{1,0:T(8,128)(2,1)} async-done(((bf16[24,2432]{1,0:T(8,128)(2,1)}), bf16[768,2432]{1,0:T(8,128)(2,1)}) %all-gather.6.cloned.1.call-update) | async-done | bytes 3735568 | tf_op jit(solution)/shard_map/all_gather | solution.py:147
  77.3 4.0 convolution_convert_fusion
  86.6 37.8 %copy.175 = pred[32,128,512]{2,0,1:T(32,128)(4,1)S(1)} copy(pred[32,128,512]{1,0,2:T(32,128)(4,1)S(1)} %iota_compare_fusion) | data formatting | bytes 4194304 | tf_op jit(solution)/shard_map/eq | solution.py:40
  136.7 9.1 %all-gather.8.cloned.1.call-done = bf16[2,4,512,768]{3,2,1,0:T(8,128)(2,1)} async-done(((bf16[2,4,128,768]{3,2,1,0:T(8,128)(2,1)}), bf16[2,4,512,768]{3,2,1,0:T(8,128)(2,1)}) %all-gather.8.cloned.1.call-update) | async-done | bytes 6291472 | tf_op jit(solution)/shard_map/all_gather | solution.py:210
  145.8 5.9 fusion.164
  154.9 5.5 copy.167
  160.4 4.8 fusion.172
  170.5 4.6 fusion.88
  176.6 82.0 %all-gather.10.cloned.1.call-done = bf16[768,10240]{1,0:T(8,128)(2,1)} async-done(((bf16[24,10240]{1,0:T(8,128)(2,1)}), bf16[768,10240]{1,0:T(8,128)(2,1)}) %all-gather.10.cloned.1.call-update) | async-done | bytes 15728656 | tf_op jit(solution)/shard_map/all_gather | solution.py:177
  260.7 5.5 reshape.352
  266.1 5.0 slice.259
  271.1 10.8 %fusion.165 = (bf16[32,24,1,768]{3,2,1,0:T(2,128)(2,1)}, bf16[32,24,1,768]{3,2,1,0:T(2,128)(2,1)}) fusion(bf16[32,24,3,768]{3,2,1,0:T(4,128)(2,1)} %reshape.352), kind=kLoop, calls=%fused_computation.274 | loop fusion | bytes 4718592 | tf_op jit(solution)/shard_map/slice | solution.py:187
  281.9 3.8 convolution_convert_fusion.7
  324.7 6.6 fusion.13
  340.9 5.6 fusion.43
  346.5 4.6 multiply_reduce_fusion.1
  353.8 5.9 multiply_convert_fusion.1
  364.3 3.8 pad_maximum_fusion.2
  379.3 7.3 fusion.40
  386.7 4.9 copy.197
  391.5 7.3 multiply_reduce_fusion
  398.8 8.6 %convert_reduce_fusion = (f32[12,128,512]{2,1,0:T(8,128)}, bf16[4,12,128,512]{3,2,1,0:T(8,128)(2,1)S(1)}) fusion(f32[4,12,128,512]{3,2,1,0:T(8,128)S(1)} %get-tuple-element.265, f32[4,12,128]{2,1,0:T(8,128)S(1)} %get-tuple-element.264, f32[4,12,128,512]{3,2,1,0:T(8,128)} %copy-done, f32[4,12,128]{2,1,0:T(8,128)S(1)} %log_add_fusion), kind=kLoop, calls=%fused_computation | loop fusion | flops 18087936 | bytes 34652160 | tf_op jit(solution)/shard_map/while/body/eval_jaxpr/reduce_sum | solution.py:361
  411.1 4.9 copy.196
  415.9 5.1 pad_maximum_fusion
  442.0 5.0 fusion.84
  453.3 6.2 fusion.90
  463.7 14.2 %reduce-scatter.7.cloned.1.call-done = bf16[2,4,128,768]{3,2,1,0:T(8,128)(2,1)} async-done(((bf16[2,4,512,768]{3,2,1,0:T(8,128)(2,1)}), bf16[2,4,128,768]{3,2,1,0:T(8,128)(2,1)}) %reduce-scatter.7.cloned.1.call-update) | async-done | bytes 1572880 | tf_op jit(solution)/shard_map/reduce_scatter | solution.py:382
  481.8 6.5 fusion.56
  503.3 14.4 %copy.219 = bf16[768,6400]{1,0:T(8,128)(2,1)} copy(bf16[768,6400]{0,1:T(8,128)(2,1)} %fusion.133) | data formatting | bytes 19660800
  517.7 6.0 add_convert_fusion
  529.5 92.2 %reduce-scatter.11.cloned.1.call-done = bf16[24,6400]{1,0:T(8,128)(2,1)} async-done(((bf16[768,6400]{1,0:T(8,128)(2,1)}), bf16[24,6400]{1,0:T(8,128)(2,1)}) %reduce-scatter.11.cloned.1.call-update) | async-done | bytes 307216 | tf_op jit(solution)/shard_map/reduce_scatter | solution.py:287
  624.9 140.2 %reduce-scatter.13.cloned.1.call-done = bf16[24,6400]{1,0:T(8,128)(2,1)} async-done(((bf16[768,6400]{1,0:T(8,128)(2,1)}), bf16[24,6400]{1,0:T(8,128)(2,1)}) %reduce-scatter.13.cloned.1.call-update) | async-done | bytes 307216
  (359 shorter events, 186.8 us)
Async XLA Ops:
  7.2 69.8 %copy-start.14 = (bf16[4,128,768]{2,1,0:T(8,128)(2,1)S(1)}, bf16[4,128,768]{2,1,0:T(8,128)(2,1)}, u32[]{:S(2)}) copy-start(bf16[4,128,768]{2,1,0:T(8,128)(2,1)} %param.20) | copy-start | bytes 2359300
  7.2 67.7 %all-gather.6.cloned.1.call-start = ((), (), s32[]{:S(2)}) async-start(), calls=%async_computation.4 | async-start | bytes 3852288 | tf_op jit(solution)/shard_map/all_gather | solution.py:147
  9.6 114.9 %all-gather.12.cloned.1.call-start = ((), (), s32[]{:S(2)}) async-start(), calls=%async_computation.10 | async-start | bytes 2457600 | tf_op jit(solution)/shard_map/all_gather | solution.py:167
  14.0 131.8 %all-gather.8.cloned.1.call-start = ((), (), s32[]{:S(2)}) async-start(), calls=%async_computation.5 | async-start | bytes 7864320 | tf_op jit(solution)/shard_map/all_gather | solution.py:210
  16.0 65.3 %copy-start.71 = (f32[512]{0:T(512)}, f32[512]{0:T(512)S(1)}, u32[]{:S(2)}) copy-start(f32[512]{0:T(512)S(1)} %get-tuple-element.251) | copy-start | bytes 6148
  76.5 298.6 %copy-start.74 = (f32[768]{0:T(1024)}, f32[768]{0:T(1024)S(1)}, u32[]{:S(2)}) copy-start(f32[768]{0:T(1024)S(1)} %get-tuple-element.211) | copy-start | bytes 9220
  82.9 175.7 %all-gather.10.cloned.1.call-start = ((), (), s32[]{:S(2)}) async-start(), calls=%async_computation.6 | async-start | bytes 16220160 | tf_op jit(solution)/shard_map/all_gather | solution.py:177
  84.0 377.8 %reduce-scatter.9.cloned.1.call-start = ((), (), s32[]{:S(2)}) async-start(), calls=%async_computation.8 | async-start | bytes 3932160 | tf_op jit(solution)/shard_map/reduce_scatter | solution.py:331
  168.1 7.0 copy-start.60
  271.1 10.8 %copy-start.39 = (bf16[4,4,64,768]{3,2,1,0:T(8,128)(2,1)S(1)}, bf16[4,4,64,768]{3,2,1,0:T(8,128)(2,1)}, u32[]{:S(2)}) copy-start(bf16[4,4,64,768]{3,2,1,0:T(8,128)(2,1)} %slice.246) | copy-start | bytes 4718596
  294.0 6.2 copy-start.15
  294.0 6.2 copy-start.28
  297.3 9.1 %copy-start.12 = (bf16[4,256,12,64]{1,0,3,2:T(4,128)(2,1)}, bf16[4,256,12,64]{1,0,3,2:T(4,128)(2,1)S(1)}, u32[]{:S(2)}) copy-start(bf16[4,256,12,64]{1,0,3,2:T(4,128)(2,1)S(1)} %squeeze.88) | copy-start | bytes 4718596
  302.5 72.6 %copy-start.79 = (f32[512]{0:T(512)}, f32[512]{0:T(512)S(1)}, u32[]{:S(2)}) copy-start(f32[512]{0:T(512)S(1)} %add_rsqrt_fusion.1) | copy-start | bytes 6148
  308.0 6.6 slice-start.2
  311.2 5.9 copy-start.41
  318.0 17.5 %copy-start.24 = (f32[512,768]{1,0:T(8,128)}, f32[512,768]{1,0:T(8,128)S(1)}, u32[]{:S(2)}) copy-start(f32[512,768]{1,0:T(8,128)S(1)} %get-tuple-element.259) | copy-start | bytes 4718596
  337.9 8.6 %slice-start = ((s8[6291456]{0:T(1024)(128)(4,1)}), s8[2097152]{0:T(1024)(128)(4,1)S(1)}, s32[]{:S(2)}) async-start(s8[6291456]{0:T(1024)(128)(4,1)} %bitcast.213), calls=%async_computation.12 | async-start | bytes 4194304
  340.9 5.6 slice-start.1
  353.8 5.9 copy-start.21
  368.1 109.8 %reduce-scatter.7.cloned.1.call-start = ((), (), s32[]{:S(2)}) async-start(), calls=%async_computation.7 | async-start | bytes 7864320 | tf_op jit(solution)/shard_map/reduce_scatter | solution.py:382
  379.3 7.3 copy-start.18
  398.8 8.6 %copy-start.19 = (bf16[4,128,12,64]{1,0,3,2:T(4,128)(2,1)S(1)}, bf16[4,128,12,64]{1,0,3,2:T(4,128)(2,1)}, u32[]{:S(2)}) copy-start(bf16[4,128,12,64]{1,0,3,2:T(4,128)(2,1)} %squeeze.84) | copy-start | bytes 2359300
  421.0 200.6 %reduce-scatter.11.cloned.1.call-start = ((), (), s32[]{:S(2)}) async-start(), calls=%async_computation.9 | async-start | bytes 10137600 | tf_op jit(solution)/shard_map/reduce_scatter | solution.py:287
  437.6 327.6 %reduce-scatter.13.cloned.1.call-start = ((), (), s32[]{:S(2)}) async-start(), calls=%async_computation.11 | async-start | bytes 10137600
  453.3 6.6 copy-start.35
  453.3 6.6 copy-start.48
  463.7 18.1 %copy-start.16 = (bf16[4,128,768]{2,1,0:T(8,128)(2,1)S(1)}, bf16[4,128,768]{2,1,0:T(8,128)(2,1)}, u32[]{:S(2)}) copy-start(bf16[4,128,768]{2,1,0:T(8,128)(2,1)} %param.20) | copy-start | bytes 2359300
  463.7 18.1 %copy-start.50 = (bf16[96,8,4,128]{3,1,2,0:T(8,128)(2,1)S(1)}, bf16[96,8,4,128]{3,1,2,0:T(8,128)(2,1)}, u32[]{:S(2)}) copy-start(bf16[96,8,4,128]{3,1,2,0:T(8,128)(2,1)} %copy.311) | copy-start | bytes 2359300
  463.7 18.1 %copy-start.72 = (f32[512]{0:T(512)S(1)}, f32[512]{0:T(512)}, u32[]{:S(2)}) copy-start(f32[512]{0:T(512)} %copy-done.71) | copy-start | bytes 6148
  479.4 8.9 %copy-start.36 = (bf16[1,4,128,768]{3,2,1,0:T(8,128)(2,1)}, bf16[1,4,128,768]{3,2,1,0:T(8,128)(2,1)S(1)}, u32[]{:S(2)}) copy-start(bf16[1,4,128,768]{3,2,1,0:T(8,128)(2,1)S(1)} %get-tuple-element.241) | copy-start | bytes 2359300
  481.8 6.6 copy-start.49
  (70 other events, 203.3 us)
Sparse Core Ops, SparseCore 0:
  11.5 63.3 all-gather.5
  77.0 20.6 all-gather.11
  99.3 46.3 all-gather.7
  148.5 110.0 all-gather.9
  368.2 36.0 reduce-scatter.8
  421.2 56.7 reduce-scatter.6
  483.9 137.7 reduce-scatter.10
  628.7 136.4 reduce-scatter.12

commit v2 on v1

--- a/solution.py
+++ b/solution.py
@@ -181,10 +181,11 @@
         pieces.append(rest_full[:, at : at + width])
         at += width
     w_out_self, c_query_w, c_key_w, c_value_w, c_out_w, f_gate, f_up = pieces
-    down_folds = rest_full[:, at:].reshape(total_devices, shard_rows, folds, model_width)
     f_down = jnp.concatenate(
         [
-            down_folds[:, : min(shard_rows, down_rows - i * shard_rows), i]
+            rest_full[:, at + i * model_width : at + (i + 1) * model_width].reshape(
+                total_devices, shard_rows, model_width
+            )[:, : min(shard_rows, down_rows - i * shard_rows)]
             for i in range(folds)
         ],
         axis=1,
@@ -284,15 +285,6 @@
         ],
         axis=1,
     )
-    ffn_summed = lax.psum_scatter(ffn_pack, axes, scatter_dimension=0, tiled=True)
-    ffn_summed = ffn_summed.astype(jnp.float32)
-    down_share = jnp.concatenate(
-        [
-            ffn_summed[:, 2 * hidden_width + i * model_width :][:, :model_width]
-            for i in range(folds)
-        ],
-        axis=0,
-    )[:down_rows]
     grad_normed_ffn = matmul_right_t(grad_gate, f_gate) + matmul_right_t(grad_up, f_up)
     grad_res_ffn, grad_g_ffn = norm_backward(grad_normed_ffn, unit_ffn, scale_ffn, g_ffn)
     grad_after_cross = grad_top + grad_res_ffn
@@ -424,8 +416,18 @@
         ],
         axis=1,
     )
-    late_summed = lax.psum_scatter(late_pack, axes, scatter_dimension=0, tiled=True)
-    late_summed = late_summed.astype(jnp.float32)
+    whole_pack = jnp.concatenate([ffn_pack, late_pack], axis=1)
+    whole_summed = lax.psum_scatter(whole_pack, axes, scatter_dimension=0, tiled=True)
+    whole_summed = whole_summed.astype(jnp.float32)
+    ffn_summed = whole_summed[:, : ffn_pack.shape[1]]
+    late_summed = whole_summed[:, ffn_pack.shape[1] :]
+    down_share = jnp.concatenate(
+        [
+            ffn_summed[:, 2 * hidden_width + i * model_width :][:, :model_width]
+            for i in range(folds)
+        ],
+        axis=0,
+    )[:down_rows]
     small_summed = late_summed[:, 8 * model_width :]
     bias_sum = small_summed[:, 3 : 3 + bias_columns].reshape(-1)[:bias_size]
     bias_grad = bias_sum.reshape(buckets_local, head_count)

time: 796 us -> 713 us (0.90)
  local copies, waits for them, and re-layouts: 188 us -> 133 us
  waiting for transfers between devices: 397 us -> 369 us
    unnamed x9 -> x7, waiting for transfers between devices: 140 us -> 0.11 us
    reduce_scatter x1, waiting for transfers between devices: 92.2 us -> 200 us  [per_device(): lax.psum_scatter(whole_pack, axes, scatter_dimension=0, tiled=True)]
    unnamed x213 -> x182, local copies, waits for them, and re-layouts: 53.5 us -> 21.7 us
    slice x5 -> x3, local copies, waits for them, and re-layouts: 19 us -> 5.94 us  [the longest x2 5.21 us: per_device(): rest_full[:, at + i * model_width:at + (i + 1) * model_width]]
  transfers between devices with their start and end apart: 8 -> 7, of which waited for: 6 -> 5; matrix products, arithmetic and copies ran while one was open for 30% -> 27% of each run, Pallas kernels for 0% -> 0%
where the time goes in v2:
time: 713 us; the launch traced here: 707 us
  waiting for transfers between devices  369 us (52%)
  matrix products  141 us (20%)
  local copies, waits for them, and re-layouts  133 us (19%)
  other arithmetic  48.8 us (7%)
  between operations  15.9 us (2%)
    reduce_scatter x1, waiting for transfers between devices, per_device(): lax.psum_scatter(whole_pack, axes, scatter_dimension=0, tiled=True)  200 us
    all_gather x1, waiting for transfers between devices, per_device(): rest_full = lax.all_gather(rest_pack, axes, axis=0, tiled=True)  82 us
    all_gather x1, waiting for transfers between devices, per_device(): first_full = lax.all_gather(first_pack, axes, axis=0, tiled=True)  58.9 us
    eq x1, local copies, waits for them, and re-layouts, bucket_table(): bucket_ids[None] == jnp.arange(NB)[:, None, None]  37.4 us
    dot_general x9, matrix products, matmul(): return jnp.dot(left, right, preferred_element_type=jnp.float32)  30.3 us
    dot_general x11, matrix products, matmul_left_t(): lax.dot_general(left, right, (((0,), (0,)), ((), ())), preferred_element_...  26.8 us
    dot_general x9, matrix products, matmul_right_t(): lax.dot_general(left, right, (((1,), (1,)), ((), ())), preferred_element_...  22.2 us
    unnamed x182, local copies, waits for them, and re-layouts  21.7 us
  transfers between devices with their start and end apart: 7, of which 5 were waited for; matrix products, arithmetic and copies ran while one was open for 27% of the time, Pallas kernels for 0%

profile of v2, /device:TPU:0, one launch (start us, length us, event | category | flops | bytes accessed | tf_op | source)
XLA Modules:
  0.0 707.5 jit_solution(15940264014279682268)
XLA Ops:
  16.0 58.9 %all-gather.6.cloned.1.call-done = bf16[768,2432]{1,0:T(8,128)(2,1)} async-done(((bf16[24,2432]{1,0:T(8,128)(2,1)}), bf16[768,2432]{1,0:T(8,128)(2,1)}) %all-gather.6.cloned.1.call-update) | async-done | bytes 3735568 | tf_op jit(solution)/shard_map/all_gather | solution.py:147
  77.3 4.0 convolution_convert_fusion
  86.6 37.4 %copy.125 = pred[32,128,512]{2,0,1:T(32,128)(4,1)S(1)} copy(pred[32,128,512]{1,0,2:T(32,128)(4,1)S(1)} %iota_compare_fusion) | data formatting | bytes 4194304 | tf_op jit(solution)/shard_map/eq | solution.py:40
  130.5 3.5 copy.126
  135.8 10.0 %all-gather.8.cloned.1.call-done = bf16[2,4,512,768]{3,2,1,0:T(8,128)(2,1)} async-done(((bf16[2,4,128,768]{3,2,1,0:T(8,128)(2,1)}), bf16[2,4,512,768]{3,2,1,0:T(8,128)(2,1)}) %all-gather.8.cloned.1.call-update) | async-done | bytes 6291472 | tf_op jit(solution)/shard_map/all_gather | solution.py:211
  145.7 5.8 fusion.157
  154.8 5.6 copy.117
  160.4 4.8 fusion.163
  170.5 4.6 fusion.88
  176.6 82.0 %all-gather.10.cloned.1.call-done = bf16[768,10240]{1,0:T(8,128)(2,1)} async-done(((bf16[24,10240]{1,0:T(8,128)(2,1)}), bf16[768,10240]{1,0:T(8,128)(2,1)}) %all-gather.10.cloned.1.call-update) | async-done | bytes 15728656 | tf_op jit(solution)/shard_map/all_gather | solution.py:177
  258.6 3.8 convolution_convert_fusion.7
  271.2 4.3 fusion.156
  301.7 6.2 fusion.13
  317.5 5.6 fusion.43
  323.1 4.9 multiply_reduce_fusion.1
  330.7 5.9 multiply_convert_fusion.1
  341.0 3.8 pad_maximum_fusion.2
  356.0 7.3 %fusion.40 = bf16[4,12,64,512]{3,2,1,0:T(8,128)(2,1)} fusion(f32[4,12,128,512]{3,2,1,0:T(8,128)} %copy-done, f32[4,12,128]{2,1,0:T(8,128)S(1)} %log_add_fusion, bf16[4,128,12,64]{1,0,3,2:T(4,128)(2,1)S(1)} %squeeze.81), kind=kOutput, calls=%fused_computation.67 | convolution fusion | flops 410517504 | bytes 16539648 | tf_op jit(solution)/shard_map/while/body/eval_jaxpr/bhqk,bqhd->bkhd/dot_general | solution.py:96
  363.3 4.8 copy.147
  368.1 7.3 %multiply_reduce_fusion = (f32[4,12,128]{2,1,0:T(8,128)S(1)}, f32[4,12,128,512]{3,2,1,0:T(8,128)S(1)}) fusion(f32[4,12,128,512]{3,2,1,0:T(8,128)} %copy-done, f32[4,12,128]{2,1,0:T(8,128)S(1)} %log_add_fusion, bf16[4,512,12,64]{1,3,2,0:T(8,128)(2,1)S(1)} %bitcast.207, bf16[4,128,12,64]{1,0,3,2:T(4,128)(2,1)} %copy-done.18), kind=kOutput, calls=%fused_computation.2 | convolution fusion | flops 412084224 | bytes 29147136 | tf_op jit(solution)/shard_map/while/body/eval_jaxpr/bqhd,bkhd->bhqk/dot_general | solution.py:79
  375.4 8.6 %convert_reduce_fusion = (f32[12,128,512]{2,1,0:T(8,128)}, bf16[4,12,128,512]{3,2,1,0:T(8,128)(2,1)S(1)}) fusion(f32[4,12,128,512]{3,2,1,0:T(8,128)S(1)} %get-tuple-element.194, f32[4,12,128]{2,1,0:T(8,128)S(1)} %get-tuple-element.193, f32[4,12,128,512]{3,2,1,0:T(8,128)} %copy-done, f32[4,12,128]{2,1,0:T(8,128)S(1)} %log_add_fusion), kind=kLoop, calls=%fused_computation | loop fusion | flops 18087936 | bytes 34652160 | tf_op jit(solution)/shard_map/while/body/eval_jaxpr/reduce_sum | solution.py:353
  387.6 4.8 copy.146
  392.4 5.1 pad_maximum_fusion
  400.7 6.1 fusion.84
  409.4 3.5 copy.162
  412.9 6.5 fusion.90
  423.5 3.6 fusion.16
  427.0 3.6 fusion.17
  437.2 17.3 %reduce-scatter.4.cloned.1.call-done = bf16[2,4,128,768]{3,2,1,0:T(8,128)(2,1)} async-done(((bf16[2,4,512,768]{3,2,1,0:T(8,128)(2,1)}), bf16[2,4,128,768]{3,2,1,0:T(8,128)(2,1)}) %reduce-scatter.4.cloned.1.call-update) | async-done | bytes 1572880 | tf_op jit(solution)/shard_map/reduce_scatter | solution.py:374
  458.6 6.1 fusion.56
  481.8 5.7 add_convert_fusion
  493.4 200.1 %reduce-scatter.8.cloned.1.call-done = bf16[24,12800]{1,0:T(8,128)(2,1)} async-done(((bf16[768,12800]{1,0:T(8,128)(2,1)}), bf16[24,12800]{1,0:T(8,128)(2,1)}) %reduce-scatter.8.cloned.1.call-update) | async-done | bytes 614416 | tf_op jit(solution)/shard_map/reduce_scatter | solution.py:420
  (321 shorter events, 149.9 us)
Async XLA Ops:
  7.2 69.8 %copy-start.14 = (bf16[4,128,768]{2,1,0:T(8,128)(2,1)S(1)}, bf16[4,128,768]{2,1,0:T(8,128)(2,1)}, u32[]{:S(2)}) copy-start(bf16[4,128,768]{2,1,0:T(8,128)(2,1)} %param.20) | copy-start | bytes 2359300
  7.2 67.7 %all-gather.6.cloned.1.call-start = ((), (), s32[]{:S(2)}) async-start(), calls=%async_computation.3 | async-start | bytes 3852288 | tf_op jit(solution)/shard_map/all_gather | solution.py:147
  9.6 114.5 %all-gather.12.cloned.1.call-start = ((), (), s32[]{:S(2)}) async-start(), calls=%async_computation.9 | async-start | bytes 2457600 | tf_op jit(solution)/shard_map/all_gather | solution.py:167
  14.0 131.8 %all-gather.8.cloned.1.call-start = ((), (), s32[]{:S(2)}) async-start(), calls=%async_computation.4 | async-start | bytes 7864320 | tf_op jit(solution)/shard_map/all_gather | solution.py:211
  16.0 65.3 %copy-start.68 = (f32[512]{0:T(512)}, f32[512]{0:T(512)S(1)}, u32[]{:S(2)}) copy-start(f32[512]{0:T(512)S(1)} %get-tuple-element.180) | copy-start | bytes 6148
  82.9 175.7 %all-gather.10.cloned.1.call-start = ((), (), s32[]{:S(2)}) async-start(), calls=%async_computation.5 | async-start | bytes 16220160 | tf_op jit(solution)/shard_map/all_gather | solution.py:177
  84.0 352.0 %reduce-scatter.6.cloned.1.call-start = ((), (), s32[]{:S(2)}) async-start(), calls=%async_computation.7 | async-start | bytes 3932160 | tf_op jit(solution)/shard_map/reduce_scatter | solution.py:323
  154.8 5.6 copy-start.3
  170.5 88.1 %copy-start.42 = (bf16[4,4,64,768]{3,2,1,0:T(8,128)(2,1)S(1)}, bf16[4,4,64,768]{3,2,1,0:T(8,128)(2,1)}, u32[]{:S(2)}) copy-start(bf16[4,4,64,768]{3,2,1,0:T(8,128)(2,1)} %slice.262) | copy-start | bytes 4718596
  271.2 13.2 %copy-start.12 = (bf16[4,256,12,64]{1,0,3,2:T(4,128)(2,1)}, bf16[4,256,12,64]{1,0,3,2:T(4,128)(2,1)S(1)}, u32[]{:S(2)}) copy-start(bf16[4,256,12,64]{1,0,3,2:T(4,128)(2,1)S(1)} %squeeze.79) | copy-start | bytes 4718596
  286.1 7.5 %slice-start.2 = ((s8[15728640]{0:T(1024)(128)(4,1)}), s8[4194304]{0:T(1024)(128)(4,1)S(1)}, s32[]{:S(2)}) async-start(s8[15728640]{0:T(1024)(128)(4,1)} %bitcast.239), calls=%async_computation.12 | async-start | bytes 8388608
  289.3 5.9 copy-start.44
  296.1 16.0 %copy-start.22 = (f32[512,768]{1,0:T(8,128)}, f32[512,768]{1,0:T(8,128)S(1)}, u32[]{:S(2)}) copy-start(f32[512,768]{1,0:T(8,128)S(1)} %get-tuple-element.188) | copy-start | bytes 4718596
  314.5 8.6 %slice-start = ((s8[6291456]{0:T(1024)(128)(4,1)}), s8[2097152]{0:T(1024)(128)(4,1)S(1)}, s32[]{:S(2)}) async-start(s8[6291456]{0:T(1024)(128)(4,1)} %bitcast.202), calls=%async_computation.10 | async-start | bytes 4194304
  317.5 5.6 slice-start.1
  317.5 5.6 copy-start.24
  330.7 5.9 copy-start.21
  344.9 109.7 %reduce-scatter.4.cloned.1.call-start = ((), (), s32[]{:S(2)}) async-start(), calls=%async_computation.6 | async-start | bytes 7864320 | tf_op jit(solution)/shard_map/reduce_scatter | solution.py:374
  356.0 7.3 %copy-start.18 = (bf16[4,128,12,64]{1,0,3,2:T(4,128)(2,1)}, bf16[4,128,12,64]{1,0,3,2:T(4,128)(2,1)S(1)}, u32[]{:S(2)}) copy-start(bf16[4,128,12,64]{1,0,3,2:T(4,128)(2,1)S(1)} %squeeze.81) | copy-start | bytes 2359300
  375.4 8.6 %copy-start.19 = (bf16[4,128,12,64]{1,0,3,2:T(4,128)(2,1)S(1)}, bf16[4,128,12,64]{1,0,3,2:T(4,128)(2,1)}, u32[]{:S(2)}) copy-start(bf16[4,128,12,64]{1,0,3,2:T(4,128)(2,1)} %squeeze.75) | copy-start | bytes 2359300
  397.5 296.0 %reduce-scatter.8.cloned.1.call-start = ((), (), s32[]{:S(2)}) async-start(), calls=%async_computation.8 | async-start | bytes 20275200 | tf_op jit(solution)/shard_map/reduce_scatter | solution.py:420
  412.9 6.9 copy-start.54
  412.9 6.9 copy-start.76
  437.2 21.4 %copy-start.16 = (bf16[4,128,768]{2,1,0:T(8,128)(2,1)S(1)}, bf16[4,128,768]{2,1,0:T(8,128)(2,1)}, u32[]{:S(2)}) copy-start(bf16[4,128,768]{2,1,0:T(8,128)(2,1)} %param.20) | copy-start | bytes 2359300
  437.2 21.4 %copy-start.69 = (f32[512]{0:T(512)S(1)}, f32[512]{0:T(512)}, u32[]{:S(2)}) copy-start(f32[512]{0:T(512)} %copy-done.68) | copy-start | bytes 6148
  456.0 8.7 %copy-start.37 = (bf16[1,4,128,768]{3,2,1,0:T(8,128)(2,1)}, bf16[1,4,128,768]{3,2,1,0:T(8,128)(2,1)S(1)}, u32[]{:S(2)}) copy-start(bf16[1,4,128,768]{3,2,1,0:T(8,128)(2,1)S(1)} %get-tuple-element.163) | copy-start | bytes 2359300
  456.0 8.7 %copy-start.39 = (bf16[1,4,128,768]{3,2,1,0:T(8,128)(2,1)}, bf16[1,4,128,768]{3,2,1,0:T(8,128)(2,1)S(1)}, u32[]{:S(2)}) copy-start(bf16[1,4,128,768]{3,2,1,0:T(8,128)(2,1)S(1)} %get-tuple-element.162) | copy-start | bytes 2359300
  465.0 6.6 copy-start.11
  465.0 6.6 copy-start.30
  473.4 5.6 copy-start.9
  473.4 5.6 copy-start.32
  693.5 5.9 copy-start.25
  (58 other events, 163.0 us)
Sparse Core Ops, SparseCore 0:
  11.5 63.3 all-gather.5
  77.0 20.7 all-gather.11
  99.3 46.3 all-gather.7
  148.5 110.0 all-gather.9
  345.0 36.1 reduce-scatter.5
  397.6 56.8 reduce-scatter.3
  481.9 211.5 reduce-scatter.7
